TPU v7x, 256 devices: a whole 4x4x8 slice. The times are simulated.
256 devices in a mesh: dp: 32 (over z_hi, y, core), tensor: 8 (over z_lo, x).
Axes of the slice: x: 4, y: 4, z: 8 (z_hi: 4, z_lo: 2; z = z_hi * 2 + z_lo), core: 2. Of those that a mesh axis runs over, the one named last changes fastest.
Arguments:
- noisy_sample: float32 [4096, 28], P('dp'), may hold values from -5 to 5
- timestep: int32 [4096], P('dp'), may hold values from 0 to 99
- noise: float32 [4096, 28], P('dp'), may hold values from -5 to 5
- obs_feat: bfloat16 [4096, 1024], P('dp'), may hold values from -6 to 6
- step_w1: bfloat16 [256, 1024], replicated, may hold values from -0.75 to 0.75
- step_w2: bfloat16 [1024, 256], replicated, may hold values from -0.25 to 0.25
- film_weight: bfloat16 [1280, 2, 4096], P('dp', None, 'tensor'), may hold values from -0.25 to 0.25
- conv_in_w: bfloat16 [5, 7, 4096], P(None, None, 'tensor'), may hold values from -1 to 1
- residual_w: bfloat16 [7, 4096], P(None, 'tensor'), may hold values from -2 to 2
- conv_mid_w: bfloat16 [5, 4096, 4096], P(None, 'dp', 'tensor'), may hold values from -0.0390625 to 0.0390625
- out_w: bfloat16 [4096, 7], P('tensor'), may hold values from -0.1875 to 0.1875
- gain_one: float32 [4096], P('tensor'), may hold values from 0.4 to 1.6
- gain_two: float32 [4096], P('tensor'), may hold values from 0.4 to 1.6
Outputs:
- predicted_noise: float32 [4096, 28], P('dp')
- denoised: float32 [4096, 28], P('dp')
All inputs are finite; a program needn't handle non-finite values.
Results may differ from a plain program's by a relative error of at most 0.0046.
Values may be sent and summed in bfloat16 or wider, within the bound.
No kernel may reach another device: no remote copies, remote signals or barrier semaphores. Data moves between devices by JAX's collectives and lax.ppermute only.
A program may use at most 192 MiB of HBM per device.

v0:
```python
import math

import jax
import jax.numpy as jnp
from jax import lax
from jax.sharding import PartitionSpec as P

C = 4096
ACT = 7
HORIZON = 4
TAPS = 5
GROUPS = 8
STEP = 256
TRAIN_STEPS = 100


def from_everyone(array, axis):
    copies = jnp.broadcast_to(array, (lax.axis_size(axis), *array.shape))
    return lax.all_to_all(copies, axis, split_axis=0, concat_axis=0, tiled=True)


def over_copies(array, axis):
    everything = from_everyone(array, axis)
    return jnp.sum(everything, axis=0)


def plan():
    pos = jnp.arange(TRAIN_STEPS + 1, dtype=jnp.float32) / TRAIN_STEPS
    curve = jnp.cos((pos + 0.008) / 1.008 * (math.pi / 2)) ** 2
    betas = jnp.minimum(1.0 - curve[1:] / curve[:-1], 0.999)
    return jnp.cumprod(1.0 - betas)


def lookup(table, steps):
    onehot = (steps[:, None] == jnp.arange(table.shape[0], dtype=jnp.int32)[None, :]).astype(
        jnp.float32
    )
    return jnp.sum(onehot * table[None, :], axis=1)


def mish(value):
    return value * jnp.tanh(jax.nn.softplus(value))


def sinusoid(steps):
    half = STEP // 2
    freqs = jnp.exp(jnp.arange(half, dtype=jnp.float32) * (-math.log(10000.0) / (half - 1)))
    angles = steps.astype(jnp.float32)[:, None] * freqs[None, :]
    return jnp.concatenate([jnp.sin(angles), jnp.cos(angles)], axis=1)


def convolve(acts, weight):
    count, length, inner = acts.shape
    padded = jnp.pad(acts, ((0, 0), (2, 2), (0, 0)))
    total = jnp.zeros((count * length, weight.shape[2]), jnp.float32)
    for shift in range(TAPS):
        window = padded[:, shift : shift + length, :].reshape(count * length, inner)
        total = total + jnp.dot(window, weight[shift], preferred_element_type=jnp.float32)
    return total.reshape(count, length, weight.shape[2])


def group_norm(hidden, gain):
    count, length, width = hidden.shape
    groups = GROUPS * width // C
    split = hidden.reshape(count, length, groups, width // groups)
    mean = jnp.mean(split, axis=(1, 3), keepdims=True)
    var = jnp.mean((split - mean) ** 2, axis=(1, 3), keepdims=True)
    normed = ((split - mean) / jnp.sqrt(var + 1e-05)).reshape(count, length, width)
    return normed * gain[None, None, :]


def denoise_step(sample, eps, noise, steps):
    alpha_bar = plan()
    now = lookup(alpha_bar, steps)[:, None]
    before = jnp.where(steps > 0, lookup(alpha_bar, jnp.maximum(steps - 1, 0)), 1.0)[:, None]
    beta_prod = 1.0 - now
    cur_alpha = now / before
    cur_beta = 1.0 - cur_alpha
    start = jnp.clip((sample - jnp.sqrt(beta_prod) * eps) / jnp.sqrt(now), -1.0, 1.0)
    mean = (
        jnp.sqrt(before) * cur_beta / beta_prod * start
        + jnp.sqrt(cur_alpha) * (1.0 - before) / beta_prod * sample
    )
    spread = jnp.sqrt((1.0 - before) / beta_prod * cur_beta)
    return mean + spread * noise


def channel_mix(acts, weight):
    rows = lax.all_gather(weight, "dp", axis=1, tiled=True)
    return convolve(lax.all_gather(acts, "tensor", axis=2, tiled=True), rows)


def body(
    noisy_sample,
    timestep,
    noise,
    obs_feat,
    step_w1,
    step_w2,
    film_weight,
    conv_in_w,
    residual_w,
    conv_mid_w,
    out_w,
    gain_one,
    gain_two,
):
    count = noisy_sample.shape[0]
    local_width = conv_in_w.shape[2]
    sample_b = noisy_sample.reshape(count, HORIZON, ACT).astype(jnp.bfloat16)
    sinus = sinusoid(timestep).astype(jnp.bfloat16)
    step_hidden = mish(jnp.dot(sinus, step_w1, preferred_element_type=jnp.float32)).astype(
        jnp.bfloat16
    )
    step_feat = jnp.dot(step_hidden, step_w2, preferred_element_type=jnp.float32)
    cond = mish(jnp.concatenate([step_feat, obs_feat.astype(jnp.float32)], axis=1)).astype(
        jnp.bfloat16
    )
    piece = lax.all_gather(film_weight, "dp", axis=0, tiled=True)
    flat = piece.reshape(piece.shape[0], 2 * local_width)
    film = jnp.dot(cond, flat, preferred_element_type=jnp.float32)
    scale = film[:, :local_width]
    shift = film[:, local_width:]
    first = mish(group_norm(convolve(sample_b, conv_in_w), gain_one))
    act_one = (scale[:, None, :] * first + shift[:, None, :]).astype(jnp.bfloat16)
    skip = jnp.dot(
        sample_b.reshape(count * HORIZON, ACT), residual_w, preferred_element_type=jnp.float32
    ).reshape(count, HORIZON, local_width)
    act_two = (mish(group_norm(channel_mix(act_one, conv_mid_w), gain_two)) + skip).astype(
        jnp.bfloat16
    )
    partial_eps = jnp.dot(
        act_two.reshape(count * HORIZON, local_width), out_w, preferred_element_type=jnp.float32
    )
    eps = over_copies(partial_eps, "tensor").reshape(count, HORIZON * ACT)
    denoised = denoise_step(noisy_sample, eps, noise, timestep)
    return (eps, denoised)


def solution(mesh):
    return jax.shard_map(
        body,
        mesh=mesh,
        in_specs=(
            P("dp", None),
            P("dp"),
            P("dp", None),
            P("dp", None),
            P(),
            P(),
            P("dp", None, "tensor"),
            P(None, None, "tensor"),
            P(None, "tensor"),
            P(None, "dp", "tensor"),
            P("tensor", None),
            P("tensor"),
            P("tensor"),
        ),
        out_specs=(P("dp", None), P("dp", None)),
        check_vma=False,
    )
```

profile of v0, /device:TPU:1, one launch (start us, length us, event | category | flops | bytes accessed | tf_op | source)
XLA Modules:
  0.0 311.4 jit_solution(10862546075395129496)
XLA Ops:
  7.2 0.7 all-gather.4.cloned.1.call-update
  8.0 0.7 convert_element_type.41
  11.0 1.0 fusion.49
  12.1 1.0 convolution_add_fusion.4
  16.5 54.2 %all-gather.4.cloned.1.call-done = bf16[1280,2,512]{2,1,0:T(2,128)(2,1)} async-done(((bf16[40,2,512]{2,1,0:T(2,128)(2,1)}), bf16[1280,2,512]{2,1,0:T(2,128)(2,1)}) %all-gather.4.cloned.1.call-update) | async-done | bytes 2621456 | tf_op jit(solution)/shard_map/all_gather | solution.py:119
  70.8 2.4 copy.115
  73.2 0.8 fusion.27
  74.1 1.8 fusion.14
  77.2 51.0 %all-gather.6.cloned.1.call-done = bf16[128,4,4096]{2,0,1:T(8,128)(2,1)} async-done(((bf16[128,4,512]{2,0,1:T(8,128)(2,1)}), bf16[128,4,4096]{2,0,1:T(8,128)(2,1)}) %all-gather.6.cloned.1.call-update) | async-done | bytes 4194320 | tf_op jit(solution)/shard_map/all_gather | solution.py:90
  128.3 8.1 %pad_slice_fusion.1 = (bf16[128,4,4096]{2,0,1:T(8,128)(2,1)}, bf16[128,4,4096]{2,0,1:T(8,128)(2,1)S(1)}, bf16[128,4,4096]{2,0,1:T(8,128)(2,1)}, bf16[128,4,4096]{2,0,1:T(8,128)(2,1)}) fusion(bf16[128,4,4096]{2,0,1:T(8,128)(2,1)} %all-gather.6.cloned.1.call-done), kind=kLoop, calls=%fused_computation.1 | loop fusion | bytes 20971520 | tf_op jit(solution)/shard_map/slice | solution.py:57
  136.4 5.2 %copy.105 = bf16[128,4,4096]{2,1,0:T(4,128)(2,1)} copy(bf16[128,4,4096]{2,0,1:T(8,128)(2,1)S(1)} %get-tuple-element.18) | data formatting | bytes 8388608 | tf_op jit(solution)/shard_map/slice | solution.py:57
  141.6 7.0 %reshape.183 = bf16[512,4096]{1,0:T(8,128)(2,1)} reshape(bf16[128,4,4096]{2,1,0:T(4,128)(2,1)} %copy.105) | data formatting | bytes 8388608 | tf_op jit(solution)/shard_map/reshape | solution.py:57
  148.6 7.4 %copy.106 = bf16[128,4,4096]{2,1,0:T(4,128)(2,1)} copy(bf16[128,4,4096]{2,0,1:T(8,128)(2,1)} %all-gather.6.cloned.1.call-done) | data formatting | bytes 8388608 | tf_op jit(solution)/shard_map/all_gather | solution.py:90
  156.0 6.9 %reshape.184 = bf16[512,4096]{1,0:T(8,128)(2,1)} reshape(bf16[128,4,4096]{2,1,0:T(4,128)(2,1)} %copy.106) | data formatting | bytes 8388608 | tf_op jit(solution)/shard_map/reshape | solution.py:57
  162.9 7.3 %copy.104 = bf16[128,4,4096]{2,1,0:T(4,128)(2,1)} copy(bf16[128,4,4096]{2,0,1:T(8,128)(2,1)} %get-tuple-element.20) | data formatting | bytes 8388608 | tf_op jit(solution)/shard_map/slice | solution.py:57
  170.3 6.9 %reshape.182 = bf16[512,4096]{1,0:T(8,128)(2,1)} reshape(bf16[128,4,4096]{2,1,0:T(4,128)(2,1)} %copy.104) | data formatting | bytes 8388608 | tf_op jit(solution)/shard_map/reshape | solution.py:57
  177.2 8.1 %copy.108 = bf16[128,4,4096]{2,1,0:T(4,128)(2,1)} copy(bf16[128,4,4096]{2,0,1:T(8,128)(2,1)} %get-tuple-element.19) | data formatting | bytes 8388608 | tf_op jit(solution)/shard_map/slice | solution.py:57
  185.3 6.9 %reshape.186 = bf16[512,4096]{1,0:T(8,128)(2,1)} reshape(bf16[128,4,4096]{2,1,0:T(4,128)(2,1)} %copy.108) | data formatting | bytes 8388608 | tf_op jit(solution)/shard_map/reshape | solution.py:57
  192.2 7.4 %copy.107 = bf16[128,4,4096]{2,1,0:T(4,128)(2,1)} copy(bf16[128,4,4096]{2,0,1:T(8,128)(2,1)} %get-tuple-element.17) | data formatting | bytes 8388608 | tf_op jit(solution)/shard_map/slice | solution.py:57
  199.7 7.0 %reshape.185 = bf16[512,4096]{1,0:T(8,128)(2,1)} reshape(bf16[128,4,4096]{2,1,0:T(4,128)(2,1)} %copy.107) | data formatting | bytes 8388608 | tf_op jit(solution)/shard_map/reshape | solution.py:57
  206.6 59.0 %all-gather.8.cloned.1.call-done = bf16[5,4096,512]{2,1,0:T(8,128)(2,1)} async-done(((bf16[5,128,512]{2,1,0:T(8,128)(2,1)}), bf16[5,4096,512]{2,1,0:T(8,128)(2,1)}) %all-gather.8.cloned.1.call-update) | async-done | bytes 20971536 | tf_op jit(solution)/shard_map/all_gather | solution.py:89
  265.7 5.9 %fusion.3 = f32[512,512]{1,0:T(8,128)S(1)} fusion(bf16[512,4096]{1,0:T(8,128)(2,1)} %reshape.183, bf16[5,4096,512]{2,1,0:T(8,128)(2,1)} %all-gather.8.cloned.1.call-done), kind=kOutput, calls=%fused_computation.11 | convolution fusion | flops 2147483648 | bytes 9437184 | tf_op jit(solution)/shard_map/dot_general | solution.py:58
  271.6 5.4 %fusion.2 = f32[512,512]{1,0:T(8,128)S(1)} fusion(bf16[512,4096]{1,0:T(8,128)(2,1)S(1)} %copy-done.2, bf16[5,4096,512]{2,1,0:T(8,128)(2,1)} %all-gather.8.cloned.1.call-done), kind=kOutput, calls=%fused_computation.9 | convolution fusion | flops 2147483648 | bytes 9437184 | tf_op jit(solution)/shard_map/dot_general | solution.py:58
  277.0 0.6 copy-done.14
  277.6 1.4 copy-done.5
  279.1 2.3 fusion
  281.4 2.3 fusion.6
  283.8 2.4 fusion.64
  287.5 1.1 fusion.9
  289.3 0.7 broadcast_in_dim.5
  290.0 8.2 %all-to-all-start = ((f32[8,512,7]{1,2,0:T(8,128)}), f32[8,512,7]{1,2,0:T(8,128)S(1)}, u32[]{:S(2)}, u32[]{:S(2)}) async-start(f32[8,512,7]{1,2,0:T(8,128)} %broadcast_in_dim.5), calls=%async_computation | async-start | bytes 262144 | tf_op jit(solution)/shard_map/all_to_all | solution.py:19
  298.2 5.6 %all-to-all-done = f32[8,512,7]{1,2,0:T(8,128)S(1)} async-done(((f32[8,512,7]{1,2,0:T(8,128)}), f32[8,512,7]{1,2,0:T(8,128)S(1)}, u32[]{:S(2)}, u32[]{:S(2)}) %all-to-all-start) | async-done | bytes 114720 | tf_op jit(solution)/shard_map/all_to_all | solution.py:19
  (96 shorter events, 10.0 us)
Async XLA Ops:
  7.2 8.7 %copy-start = (bf16[1024,256]{1,0:T(8,128)(2,1)S(1)}, bf16[1024,256]{1,0:T(8,128)(2,1)}, u32[]{:S(2)}) copy-start(bf16[1024,256]{1,0:T(8,128)(2,1)} %param.18) | copy-start | bytes 1572868
  7.2 5.9 %copy-start.9 = (bf16[5,7,512]{2,1,0:T(8,128)(2,1)S(1)}, bf16[5,7,512]{2,1,0:T(8,128)(2,1)}, u32[]{:S(2)}) copy-start(bf16[5,7,512]{2,1,0:T(8,128)(2,1)} %param.20) | copy-start | bytes 107524
  7.2 63.6 %all-gather.4.cloned.1.call-start = ((), (), s32[]{:S(2)}) async-start(), calls=%async_computation.1 | async-start | bytes 2703360 | tf_op jit(solution)/shard_map/all_gather | solution.py:119
  7.9 120.4 %all-gather.6.cloned.1.call-start = ((), (), s32[]{:S(2)}) async-start(), calls=%async_computation.2 | async-start | bytes 4718592 | tf_op jit(solution)/shard_map/all_gather | solution.py:90
  13.4 2.1 copy-start.6
  13.4 2.1 copy-start.13
  13.4 2.5 copy-start.15
  70.7 3.3 %copy-start.12 = (f32[512]{0:T(512)S(1)}, f32[512]{0:T(512)}, u32[]{:S(2)}) copy-start(f32[512]{0:T(512)} %param.24) | copy-start | bytes 6148
  75.9 189.8 %all-gather.8.cloned.1.call-start = ((), (), s32[]{:S(2)}) async-start(), calls=%async_computation.3 | async-start | bytes 21626880 | tf_op jit(solution)/shard_map/all_gather | solution.py:89
  265.7 5.9 %copy-start.2 = (bf16[512,4096]{1,0:T(8,128)(2,1)S(1)}, bf16[512,4096]{1,0:T(8,128)(2,1)}, u32[]{:S(2)}) copy-start(bf16[512,4096]{1,0:T(8,128)(2,1)} %reshape.184) | copy-start | bytes 12582916
  265.7 12.0 %copy-start.14 = (bf16[5,4096,512]{2,1,0:T(8,128)(2,1)S(1)}, bf16[5,4096,512]{2,1,0:T(8,128)(2,1)}, u32[]{:S(2)}) copy-start(bf16[5,4096,512]{2,1,0:T(8,128)(2,1)} %all-gather.8.cloned.1.call-done) | copy-start | bytes 62914564
  271.6 7.4 %copy-start.5 = (bf16[512,4096]{1,0:T(8,128)(2,1)S(1)}, bf16[512,4096]{1,0:T(8,128)(2,1)}, u32[]{:S(2)}) copy-start(bf16[512,4096]{1,0:T(8,128)(2,1)} %reshape.186) | copy-start | bytes 12582916
  279.0 2.3 copy-start.3
  281.4 2.3 copy-start.4
  283.7 3.7 %copy-start.16 = (bf16[7,512]{1,0:T(8,128)(2,1)S(1)}, bf16[7,512]{1,0:T(8,128)(2,1)}, u32[]{:S(2)}) copy-start(bf16[7,512]{1,0:T(8,128)(2,1)} %param.21) | copy-start | bytes 21508
  283.8 3.7 %copy-start.17 = (f32[512]{0:T(512)S(1)}, f32[512]{0:T(512)}, u32[]{:S(2)}) copy-start(f32[512]{0:T(512)} %param.25) | copy-start | bytes 6148
  287.4 17.4 %copy-start.1 = (bf16[1024,256]{1,0:T(8,128)(2,1)S(1)}, bf16[1024,256]{1,0:T(8,128)(2,1)}, u32[]{:S(2)}) copy-start(bf16[1024,256]{1,0:T(8,128)(2,1)} %param.18) | copy-start | bytes 1572868
  287.5 1.7 copy-start.11
  287.5 16.7 %copy-start.8 = (f32[128,28]{0,1:T(8,128)S(1)}, f32[128,28]{0,1:T(8,128)}, u32[]{:S(2)}) copy-start(f32[128,28]{0,1:T(8,128)} %param.13) | copy-start | bytes 43012
  287.5 16.7 %copy-start.10 = (f32[128,28]{0,1:T(8,128)S(1)}, f32[128,28]{0,1:T(8,128)}, u32[]{:S(2)}) copy-start(f32[128,28]{0,1:T(8,128)} %param.15) | copy-start | bytes 43012
  290.0 13.8 %all-to-all-start = ((f32[8,512,7]{1,2,0:T(8,128)}), f32[8,512,7]{1,2,0:T(8,128)S(1)}, u32[]{:S(2)}, u32[]{:S(2)}) async-start(f32[8,512,7]{1,2,0:T(8,128)} %broadcast_in_dim.5), calls=%async_computation | async-start | bytes 262144 | tf_op jit(solution)/shard_map/all_to_all | solution.py:19
  304.2 0.7 copy-start.7
Sparse Core Ops, SparseCore 0:
  10.6 60.1 all-gather.3
  76.0 52.2 all-gather.5
  130.9 134.7 all-gather.7
where the time goes:
time: 313 us; the launch traced here: 311 us
  waiting for transfers between devices  171 us (55%)
  local copies, waits for them, and re-layouts  88.4 us (28%)
  matrix products  24.2 us (8%)
  between operations  14.3 us (5%)
  starting transfers between devices  8.47 us (3%)
  other arithmetic  4.97 us (2%)
    all_gather x1, waiting for transfers between devices, channel_mix(): rows = lax.all_gather(weight, 'dp', axis=1, tiled=True)  59 us
    all_gather x1, waiting for transfers between devices, body(): piece = lax.all_gather(film_weight, 'dp', axis=0, tiled=True)  54.2 us
    all_gather x1, waiting for transfers between devices, channel_mix(): return convolve(lax.all_gather(acts, 'tensor', axis=2, tiled=True), rows)  51 us
    slice x10, local copies, waits for them, and re-layouts, convolve(): window = padded[:, shift:shift + length, :].reshape(count * length, inner)  37 us
    reshape x9, local copies, waits for them, and re-layouts, convolve(): window = padded[:, shift:shift + length, :].reshape(count * length, inner)  36 us
    dot_general x10, matrix products, convolve(): jnp.dot(window, weight[shift], preferred_element_type=jnp.float32)  21.5 us
    all_to_all x1, starting transfers between devices, from_everyone(): return lax.all_to_all(copies, axis, split_axis=0, concat_axis=0, tiled=True)  8.17 us
    all_gather x1, local copies, waits for them, and re-layouts, channel_mix(): return convolve(lax.all_gather(acts, 'tensor', axis=2, tiled=True), rows)  7.4 us
  transfers between devices with their start and end apart: 4, of which 4 were waited for; matrix products, arithmetic and copies ran while one was open for 28% of the time, Pallas kernels for 0%

commit v1 on v0

v1 whole, which is shorter than its diff:
```python
import math

import jax
import jax.numpy as jnp
import numpy as np
from jax import lax
from jax.experimental import pallas as pl
from jax.experimental.pallas import tpu as pltpu
from jax.sharding import Mesh, PartitionSpec as P

C = 4096
ACT = 7
HORIZON = 4
TAPS = 5
GROUPS = 8
STEP = 256
TRAIN_STEPS = 100
COND = 1280

AXES = ("zq", "zp", "y", "core", "zl", "x")
SIZES = (2, 2, 4, 2, 2, 4)
DP = ("zq", "zp", "y", "core")
TENSOR = ("zl", "x")

OWN = 128
PAIR = 256
ROWS = HORIZON * PAIR
WIDE = 512
HALF = 256
WIN = 48
FILM_ROWS = 2 * PAIR + WIN

f32, bf16 = jnp.float32, jnp.bfloat16


def moves(where):
    pairs = []
    for here in np.ndindex(*SIZES):
        zq, zp, y, core, zl, x = here
        zh, y, core, zl, x = where(2 * zq + zp, y, core, zl, x)
        there = ((zh % 4) // 2, zh % 2, y % 4, core % 2, zl % 2, x % 4)
        pairs.append(
            (int(np.ravel_multi_index(here, SIZES)), int(np.ravel_multi_index(there, SIZES)))
        )
    return pairs


def mover(where):
    pairs = moves(where)
    return lambda array: lax.ppermute(array, AXES, pairs)


z_up = mover(lambda zh, y, core, zl, x: (zh + 1, y, core, zl, x))
z_down = mover(lambda zh, y, core, zl, x: (zh - 1, y, core, zl, x))
z_two = mover(lambda zh, y, core, zl, x: (zh + 2, y, core, zl, x))
z_pair = mover(lambda zh, y, core, zl, x: (zh ^ 1, y, core, zl, x))
y_up = mover(lambda zh, y, core, zl, x: (zh, y + 1, core, zl, x))
y_down = mover(lambda zh, y, core, zl, x: (zh, y - 1, core, zl, x))
cores = mover(lambda zh, y, core, zl, x: (zh, y, 1 - core, zl, x))
zl_swap = mover(lambda zh, y, core, zl, x: (zh, y, core, 1 - zl, x))
x_ring = mover(lambda zh, y, core, zl, x: (zh, y, core, zl, x + 1 - 2 * core))


def plan():
    pos = np.arange(TRAIN_STEPS + 1, dtype=np.float64) / TRAIN_STEPS
    curve = np.cos((pos + 0.008) / 1.008 * (math.pi / 2)) ** 2
    betas = np.minimum(1.0 - curve[1:] / curve[:-1], 0.999)
    return jnp.asarray(np.cumprod(1.0 - betas), f32)


def lookup(table, steps):
    onehot = (steps[:, None] == jnp.arange(table.shape[0], dtype=jnp.int32)[None, :]).astype(f32)
    return jnp.sum(onehot * table[None, :], axis=1)


def mish(value):
    return value * jnp.tanh(jax.nn.softplus(value))


def mish_by_exp(value):
    u = jnp.exp(jnp.minimum(value, 20.0))
    w = u * (u + 2.0)
    return value * (w / (w + 2.0))


def sinusoid(steps):
    half = STEP // 2
    freqs = jnp.exp(jnp.arange(half, dtype=f32) * (-math.log(10000.0) / (half - 1)))
    angles = steps.astype(f32)[:, None] * freqs[None, :]
    return jnp.concatenate([jnp.sin(angles), jnp.cos(angles)], axis=1)


def denoise_coefficients(steps):
    alpha_bar = plan()
    now = lookup(alpha_bar, steps)[:, None]
    before = jnp.where(steps > 0, lookup(alpha_bar, jnp.maximum(steps - 1, 0)), 1.0)[:, None]
    beta_prod = 1.0 - now
    cur_alpha = now / before
    cur_beta = 1.0 - cur_alpha
    return (
        jnp.sqrt(beta_prod),
        jnp.sqrt(now),
        jnp.sqrt(before) * cur_beta / beta_prod,
        jnp.sqrt(cur_alpha) * (1.0 - before) / beta_prod,
        jnp.sqrt((1.0 - before) / beta_prod * cur_beta),
    )


def params(mib, **more):
    return pltpu.CompilerParams(vmem_limit_bytes=mib * 2**20, **more)


def film_kernel(order_ref, cond_ref, mine_ref, sibling_ref, small_ref, out_ref):
    core = order_ref[16]
    mine = jnp.zeros((PAIR, WIDE), f32)
    other = jnp.zeros((PAIR, WIDE), f32)
    for r in range(16):
        rows = cond_ref[order_ref[r]]
        mine += jnp.dot(rows, mine_ref[r], preferred_element_type=f32)
        other += jnp.dot(rows, sibling_ref[r], preferred_element_type=f32)
    out_ref[pl.ds(pl.multiple_of(core * PAIR, PAIR), PAIR), :] = mine.astype(bf16)
    out_ref[pl.ds(pl.multiple_of((1 - core) * PAIR, PAIR), PAIR), :] = other.astype(bf16)
    out_ref[2 * PAIR :, :] = small_ref[...]


def film_of(order, cond_blocks, mine, sibling, small):
    return pl.pallas_call(
        film_kernel,
        out_shape=jax.ShapeDtypeStruct((FILM_ROWS, WIDE), bf16),
        in_specs=[pl.BlockSpec(memory_space=pltpu.SMEM)]
        + [pl.BlockSpec(memory_space=pltpu.VMEM)] * 4,
        out_specs=pl.BlockSpec(memory_space=pltpu.VMEM),
        compiler_params=params(24),
        cost_estimate=pl.CostEstimate(
            flops=2 * PAIR * COND * 2 * WIDE, bytes_accessed=4 * 2**20, transcendentals=0
        ),
        name="film",
    )(order, cond_blocks, mine, sibling, small)


def first_kernel(place_ref, window_ref, film_ref, *rest):
    out_ref, hidden_ref = rest[-2:]
    hidden_ref[...] = jnp.dot(
        window_ref[...], film_ref[2 * PAIR :, :], preferred_element_type=f32
    )
    gain = (
        film_ref[2 * PAIR + 35 : 2 * PAIR + 36, :].astype(f32)
        + film_ref[2 * PAIR + 36 : 2 * PAIR + 37, :].astype(f32)
    )
    some = 16

    @pl.loop(0, PAIR // some)
    def _(step):
        at = [pl.multiple_of(p * PAIR + step * some, some) for p in range(HORIZON)]
        hidden = [hidden_ref[pl.ds(a, some), :] for a in at]
        mean = jnp.sum(sum(hidden), axis=1, keepdims=True) * (1.0 / (HORIZON * WIDE))
        off = [h - mean for h in hidden]
        var = jnp.sum(sum(o * o for o in off), axis=1, keepdims=True) * (1.0 / (HORIZON * WIDE))
        inv = lax.rsqrt(var + 1e-05)
        scale = film_ref[pl.ds(at[0], some), :].astype(f32)
        shift = film_ref[pl.ds(at[1], some), :].astype(f32)
        for a, o in zip(at, off):
            out_ref[0, pl.ds(a, some), :] = (
                scale * mish_by_exp(o * inv * gain) + shift
            ).astype(bf16)


def first_of(place, window, film, before):
    more = [] if before is None else [before]
    return pl.pallas_call(
        first_kernel,
        out_shape=jax.ShapeDtypeStruct((8, ROWS, WIDE), bf16),
        grid_spec=pltpu.PrefetchScalarGridSpec(
            num_scalar_prefetch=1,
            grid=(1,),
            in_specs=[
                pl.BlockSpec((ROWS, WIN), lambda i, place: (0, 0)),
                pl.BlockSpec((FILM_ROWS, WIDE), lambda i, place: (0, 0)),
            ]
            + [pl.BlockSpec(memory_space=pl.ANY)] * len(more),
            out_specs=pl.BlockSpec((1, ROWS, WIDE), lambda i, place: (place[0], 0, 0)),
            scratch_shapes=[pltpu.VMEM((ROWS, WIDE), f32)],
        ),
        input_output_aliases={3: 0} if more else {},
        compiler_params=params(24),
        cost_estimate=pl.CostEstimate(
            flops=2 * ROWS * WIN * WIDE, bytes_accessed=2 * 2**20, transcendentals=ROWS * WIDE
        ),
        name="first",
    )(place, window, film, *more)


def mid_kernel(stats, place_ref, act_ref, weight_ref, *rest):
    rest = list(rest)
    stats_ref = rest.pop() if stats else None
    out_ref = rest.pop()
    j, q = pl.program_id(0), pl.program_id(1)

    @pl.when(jnp.logical_and(j == 0, q == 0))
    def _():
        out_ref[...] = rest[0][...] if rest else jnp.zeros_like(out_ref)

    for h in range(HORIZON):
        total = out_ref[h * PAIR : (h + 1) * PAIR, :]
        for p in range(HORIZON):
            k = p - h + 2
            if 0 <= k < TAPS:
                total += jnp.dot(
                    act_ref[0, p * PAIR : (p + 1) * PAIR, :],
                    weight_ref[:, 0, k].reshape(WIDE, HALF),
                    preferred_element_type=f32,
                )
        out_ref[h * PAIR : (h + 1) * PAIR, :] = total

    if stats:

        @pl.when(jnp.logical_and(j == pl.num_programs(0) - 1, q == 1))
        def _():
            parts = [out_ref[h * PAIR : (h + 1) * PAIR, :] for h in range(HORIZON)]
            mean = jnp.sum(sum(parts), axis=1, keepdims=True) * (1.0 / (HORIZON * HALF))
            spread = jnp.sum(sum((o - mean) ** 2 for o in parts), axis=1, keepdims=True)
            lane = lax.broadcasted_iota(jnp.int32, (PAIR, 128), 1)
            both = jnp.where(lane == 0, mean, jnp.where(lane == 1, spread, 0.0))
            stats_ref[...] = both.T[:8, :]


def mid_of(place, acts, weights, before, stats):
    pieces = weights.shape[1]
    more = [] if before is None else [before]
    whole = pl.BlockSpec((ROWS, HALF), lambda j, q, place: (0, 0))
    out_shape = [jax.ShapeDtypeStruct((ROWS, HALF), f32)]
    out_specs = [whole]
    if stats:
        out_shape.append(jax.ShapeDtypeStruct((8, PAIR), f32))
        out_specs.append(pl.BlockSpec((8, PAIR), lambda j, q, place: (0, 0)))

    def kernel(*refs):
        mid_kernel(stats, *refs)

    return pl.pallas_call(
        kernel,
        out_shape=out_shape,
        grid_spec=pltpu.PrefetchScalarGridSpec(
            num_scalar_prefetch=1,
            grid=(pieces, 2),
            in_specs=[
                pl.BlockSpec((1, ROWS, WIDE), lambda j, q, place: (place[2 * j + q], 0, 0)),
                pl.BlockSpec(
                    (4, 1, TAPS, OWN, HALF), lambda j, q, place: (q, j, 0, 0, 0)
                ),
            ]
            + [whole] * len(more),
            out_specs=out_specs,
        ),
        compiler_params=params(28),
        cost_estimate=pl.CostEstimate(
            flops=2 * pieces * 2 * 14 * PAIR * WIDE * HALF,
            bytes_accessed=pieces * 5 * 2**20,
            transcendentals=0,
        ),
        name="mid",
    )(place, acts, weights, *more)


def last_kernel(conv_ref, own_ref, other_ref, gain_ref, window_ref, res_ref, out_w_ref, eps_ref):
    rows = jnp.concatenate([own_ref[...], other_ref[...], jnp.zeros((112, PAIR), f32)], axis=0).T
    mean_a, spread_a = rows[:, 0:1], rows[:, 1:2]
    mean_b, spread_b = rows[:, 8:9], rows[:, 9:10]
    each = HORIZON * HALF
    mean = 0.5 * (mean_a + mean_b)
    var = (spread_a + spread_b + (mean_a - mean_b) ** 2 * (0.5 * each)) * (0.5 / each)
    inv = lax.rsqrt(var + 1e-05)
    total = jnp.zeros((32, PAIR), f32)
    for h in range(HORIZON):
        at = slice(h * PAIR, (h + 1) * PAIR)
        normed = (conv_ref[at, :] - mean) * inv * gain_ref[...]
        skip = jnp.dot(window_ref[at, :], res_ref[...], preferred_element_type=f32)
        act = (mish_by_exp(normed) + skip).astype(bf16)
        total += lax.dot_general(
            out_w_ref[h], act, (((1,), (1,)), ((), ())), preferred_element_type=f32
        )
    eps_ref[0] = total[:, :OWN]
    eps_ref[1] = total[:, OWN:]


def last_of(conv, own, other, gain, window, res, out_w):
    return pl.pallas_call(
        last_kernel,
        out_shape=jax.ShapeDtypeStruct((2, 32, OWN), f32),
        in_specs=[pl.BlockSpec(memory_space=pltpu.VMEM)] * 7,
        out_specs=pl.BlockSpec(memory_space=pltpu.VMEM),
        compiler_params=params(24),
        cost_estimate=pl.CostEstimate(
            flops=2 * ROWS * HALF * 80, bytes_accessed=2 * 2**20, transcendentals=ROWS * HALF
        ),
        name="last",
    )(conv, own, other, gain, window, res, out_w)


def body(
    noisy_sample,
    timestep,
    noise,
    obs_feat,
    step_w1,
    step_w2,
    film_weight,
    conv_in_w,
    residual_w,
    conv_mid_w,
    out_w,
    gain_one,
    gain_two,
):
    zq, zp, y, core, zl, x = (lax.axis_index(a) for a in AXES)
    zh = 2 * zq + zp

    keep = lax.dynamic_slice_in_dim(conv_mid_w, zp * HALF, HALF, 2)
    give = lax.dynamic_slice_in_dim(conv_mid_w, (1 - zp) * HALF, HALF, 2)
    w_own = lax.all_gather(keep[None], ("y", "core"), axis=0, tiled=False)
    w_rest = jnp.stack([z_up(give), z_down(give), z_two(keep)])
    w_rest = lax.all_gather(w_rest, ("y", "core"), axis=0, tiled=False)

    stay = lax.dynamic_index_in_dim(film_weight, core, 1, keepdims=False)
    go = lax.dynamic_index_in_dim(film_weight, 1 - core, 1, keepdims=False)
    come = cores(go)
    chip = jnp.where(
        core == 0, jnp.concatenate([stay, come]), jnp.concatenate([come, stay])
    )
    line = jnp.stack([chip, z_up(chip), z_down(chip), z_two(chip)])
    from_down, from_up = y_up(line), y_down(line)
    far_a, far_b = y_up(from_down[:2]), y_down(from_up[2:])
    mine = jnp.concatenate([line, from_down, from_up, far_a, far_b])
    sibling = cores(mine)
    dz = (0, -1, 1, 2)
    order = [((zh + dz[r % 4]) % 4) * 4 + (y + dy) % 4 for dy in (0, -1, 1, 2) for r in range(4)]
    order = jnp.stack(order + [core]).astype(jnp.int32)

    sample_b = noisy_sample.astype(bf16)
    sinus = sinusoid(timestep).astype(bf16)
    step_hidden = mish(jnp.dot(sinus, step_w1, preferred_element_type=f32)).astype(bf16)
    step_feat = jnp.dot(step_hidden, step_w2, preferred_element_type=f32)
    cond = mish(jnp.concatenate([step_feat, obs_feat.astype(f32)], axis=1)).astype(bf16)
    packed = jnp.concatenate([cond, jnp.pad(sample_b, ((0, 0), (0, 100)))], axis=1)
    partner = z_pair(packed)
    both = jnp.where(
        zp == 0, jnp.concatenate([packed, partner]), jnp.concatenate([partner, packed])
    )
    cond_blocks = both[:, :COND].reshape(PAIR, 16, 80).transpose(1, 0, 2)
    samples = jnp.pad(both[:, COND : COND + 28], ((0, 0), (14, 14)))
    window = jnp.concatenate([samples[:, 7 * p : 7 * p + 35] for p in range(HORIZON)])
    window = jnp.pad(window, ((0, 0), (0, WIN - 35)))

    coarse = lax.reduce_precision(gain_one, 8, 7)
    small = jnp.concatenate(
        [
            conv_in_w.reshape(TAPS * ACT, WIDE),
            coarse[None].astype(bf16),
            (gain_one - coarse)[None].astype(bf16),
            jnp.zeros((WIN - 37, WIDE), bf16),
        ]
    )
    film = film_of(order, cond_blocks, mine, sibling, small)

    a, b = [film], [zl_swap(film)]
    for _ in range(3):
        a.append(x_ring(a[-1]))
        b.append(x_ring(b[-1]))
    acts = None
    for side, step in ((0, 0), (0, 1), (1, 0), (0, 2), (1, 1), (0, 3), (1, 2), (1, 3)):
        owner = (x + step * (2 * core - 1)) % 4
        block = jnp.where(side == 0, zl, 1 - zl) * 4 + owner
        acts = first_of(
            block.reshape(1).astype(jnp.int32), window, (a if side == 0 else b)[step], acts
        )

    def blocks(*shifts):
        return jnp.stack([((zh + s) % 4) * 2 + q for s in shifts for q in range(2)]).astype(jnp.int32)

    [conv] = mid_of(blocks(0), acts, w_own, None, False)
    conv, stats = mid_of(blocks(-1, 1, 2), acts, w_rest, conv, True)
    other = z_pair(stats)

    out_h = lax.dynamic_slice_in_dim(out_w, zp * HALF, HALF, 0).T
    out_h = jnp.stack([jnp.pad(out_h, ((7 * h, 25 - 7 * h), (0, 0))) for h in range(HORIZON)])
    res_h = lax.dynamic_slice_in_dim(residual_w, zp * HALF, HALF, 1)
    res_h = jnp.pad(res_h, ((14, WIN - 21), (0, 0)))
    gain_h = lax.dynamic_slice_in_dim(gain_two, zp * HALF, HALF, 0)[None]
    part = last_of(conv, stats, other, gain_h, window, res_h, out_h)

    sent = jnp.broadcast_to(part[:, None], (2, 8, 32, OWN)).reshape(16, 32, OWN)
    got = lax.all_to_all(sent, ("zp", "zl", "x"), split_axis=0, concat_axis=0, tiled=True)
    eps = jnp.sum(got, axis=0).T[:, :28]

    root_b, root_a, of_start, of_sample, of_noise = denoise_coefficients(timestep)
    start = jnp.clip((noisy_sample - root_b * eps) / root_a, -1.0, 1.0)
    denoised = of_start * start + of_sample * noisy_sample + of_noise * noise
    return (eps, denoised)


def solution(mesh):
    fine = Mesh(mesh.devices.reshape(SIZES), AXES)
    return jax.shard_map(
        body,
        mesh=fine,
        in_specs=(
            P(DP, None),
            P(DP),
            P(DP, None),
            P(DP, None),
            P(),
            P(),
            P(DP, None, TENSOR),
            P(None, None, TENSOR),
            P(None, TENSOR),
            P(None, DP, TENSOR),
            P(TENSOR, None),
            P(TENSOR),
            P(TENSOR),
        ),
        out_specs=(P(DP, None), P(DP, None)),
        check_vma=False,
    )
```

time: 313 us -> 258 us (0.82)
  waiting for transfers between devices: 171 us -> 94 us
  local copies, waits for them, and re-layouts: 88.4 us -> 23.1 us
  Pallas kernels: 0 us -> 54.5 us
  starting transfers between devices: 8.47 us -> 62.1 us
  matrix products: 24.2 us -> 1.81 us
    all_gather x3 -> x2, waiting for transfers between devices: 164 us -> 0.02 us  [the longest x1 0.02 us: body(): w_rest = lax.all_gather(w_rest, ('y', 'core'), axis=0, tiled=False)]
    ppermute x0 -> x21, waiting for transfers between devices: none -> 85.2 us  [mover(): return lambda array: lax.ppermute(array, AXES, pairs)]
    ppermute x0 -> x21, starting transfers between devices: none -> 57.5 us  [mover(): return lambda array: lax.ppermute(array, AXES, pairs)]
    pallas_call x0 -> x12, Pallas kernels: none -> 54.5 us  [the longest x8 38.8 us: first_of(): pl.pallas_call(first_kernel, out_shape=jax.ShapeDtypeStruct((8, ROWS, WID...]
    slice x11 -> x6, local copies, waits for them, and re-layouts: 37.1 us -> 1.01 us  [the longest x1 0.96 us: body(): cond_blocks = both[:, :COND].reshape(PAIR, 16, 80).transpose(1, 0, 2)]
    reshape x11 -> x2, local copies, waits for them, and re-layouts: 36.2 us -> 1.57 us  [the longest x1 1.55 us: body(): cond_blocks = both[:, :COND].reshape(PAIR, 16, 80).transpose(1, 0, 2)]
    dot_general x14 -> x1, matrix products: 24.2 us -> 1.81 us  [body(): step_feat = jnp.dot(step_hidden, step_w2, preferred_element_type=f32)]
    unnamed x38 -> x47, local copies, waits for them, and re-layouts: 4.68 us -> 15.4 us
  transfers between devices with their start and end apart: 4 -> 24, of which waited for: 4 -> 14; matrix products, arithmetic and copies ran while one was open for 28% -> 4% of each run, Pallas kernels for 0% -> 18%
where the time goes in v1:
time: 258 us; the launch traced here: 254 us
  waiting for transfers between devices  94 us (36%)
  starting transfers between devices  62.1 us (24%)
  Pallas kernels  54.5 us (21%)
  local copies, waits for them, and re-layouts  23.1 us (9%)
  between operations  14.6 us (6%)
  other arithmetic  3.67 us (1%)
    ppermute x21, waiting for transfers between devices, mover(): return lambda array: lax.ppermute(array, AXES, pairs)  85.2 us
    ppermute x21, starting transfers between devices, mover(): return lambda array: lax.ppermute(array, AXES, pairs)  57.5 us
    pallas_call x8, Pallas kernels, first_of(): pl.pallas_call(first_kernel, out_shape=jax.ShapeDtypeStruct((8, ROWS, WID...  38.8 us
    unnamed x47, local copies, waits for them, and re-layouts  15.4 us
    pallas_call x2, Pallas kernels, mid_of(): pl.pallas_call(kernel, out_shape=out_shape, grid_spec=pltpu.PrefetchScala...  11.1 us
    all_to_all x1, waiting for transfers between devices, body(): lax.all_to_all(sent, ('zp', 'zl', 'x'), split_axis=0, concat_axis=0, tile...  8.78 us
  transfers between devices with their start and end apart: 24, of which 14 were waited for; matrix products, arithmetic and copies ran while one was open for 4% of the time, Pallas kernels for 18%

profile of v1, /device:TPU:1, one launch (start us, length us, event | category | flops | bytes accessed | tf_op | source)
XLA Modules:
  0.0 253.8 jit_solution(1040495105703547266)
XLA Ops:
  9.2 3.9 %collective-permute-start.17 = (bf16[5,128,256]{2,1,0:T(8,128)(2,1)S(1)}, bf16[5,128,256]{2,1,0:T(8,128)(2,1)S(1)}, u32[]{:S(2)}, u32[]{:S(2)}) collective-permute-start(bf16[5,128,256]{2,1,0:T(8,128)(2,1)S(1)} %get-tuple-element.15), channel_id=1, source_target_pairs={{0,64},{1,65},{2,66},{3,67},{4,68},{5,69},{6,70},{7,71},{8,72},{9,... | collective-permute-start | bytes 983048 | tf_op jit(solution)/shard_map/ppermute | solution.py:50
  13.1 3.1 %collective-permute-start.18 = (bf16[5,128,256]{2,1,0:T(8,128)(2,1)S(1)}, bf16[5,128,256]{2,1,0:T(8,128)(2,1)S(1)}, u32[]{:S(2)}, u32[]{:S(2)}) collective-permute-start(bf16[5,128,256]{2,1,0:T(8,128)(2,1)S(1)} %get-tuple-element.15), channel_id=1, source_target_pairs={{0,192},{1,193},{2,194},{3,195},{4,196},{5,197},{6,198},{7,199},{8... | collective-permute-start | bytes 983048 | tf_op jit(solution)/shard_map/ppermute | solution.py:50
  16.2 4.4 %collective-permute-start.19 = (bf16[5,128,256]{2,1,0:T(8,128)(2,1)}, bf16[5,128,256]{2,1,0:T(8,128)(2,1)S(1)}, u32[]{:S(2)}, u32[]{:S(2)}) collective-permute-start(bf16[5,128,256]{2,1,0:T(8,128)(2,1)} %get-tuple-element.16), channel_id=1, source_target_pairs={{0,128},{1,129},{2,130},{3,131},{4,132},{5,133},{6,134},{7,135},{8... | collective-permute-start | bytes 983048 | tf_op jit(solution)/shard_map/ppermute | solution.py:50
  20.6 5.0 %collective-permute-done.17 = bf16[5,128,256]{2,1,0:T(8,128)(2,1)S(1)} collective-permute-done((bf16[5,128,256]{2,1,0:T(8,128)(2,1)S(1)}, bf16[5,128,256]{2,1,0:T(8,128)(2,1)S(1)}, u32[]{:S(2)}, u32[]{:S(2)}) %collective-permute-start.17) | collective-permute-done | bytes 327712 | tf_op jit(solution)/shard_map/ppermute | solution.py:50
  25.6 14.3 %collective-permute-done.18 = bf16[5,128,256]{2,1,0:T(8,128)(2,1)S(1)} collective-permute-done((bf16[5,128,256]{2,1,0:T(8,128)(2,1)S(1)}, bf16[5,128,256]{2,1,0:T(8,128)(2,1)S(1)}, u32[]{:S(2)}, u32[]{:S(2)}) %collective-permute-start.18) | collective-permute-done | bytes 327712 | tf_op jit(solution)/shard_map/ppermute | solution.py:50
  43.4 9.9 %collective-permute-start.2 = (bf16[80,512]{1,0:T(8,128)(2,1)S(1)}, bf16[80,512]{1,0:T(8,128)(2,1)S(1)}, u32[]{:S(2)}, u32[]{:S(2)}) collective-permute-start(bf16[80,512]{1,0:T(8,128)(2,1)S(1)} %maximum_select_fusion.2), channel_id=1, source_target_pairs={{0,64},{1,65},{2,66},{3,67},{4,68},{5,69},{6,70},{7,71},{8,72},{9,... | collective-permute-start | bytes 245768 | tf_op jit(solution)/shard_map/ppermute | solution.py:50
  53.2 3.4 %collective-permute-start.4 = (bf16[80,512]{1,0:T(8,128)(2,1)S(1)}, bf16[80,512]{1,0:T(8,128)(2,1)S(1)}, u32[]{:S(2)}, u32[]{:S(2)}) collective-permute-start(bf16[80,512]{1,0:T(8,128)(2,1)S(1)} %maximum_select_fusion.2), channel_id=1, source_target_pairs={{0,128},{1,129},{2,130},{3,131},{4,132},{5,133},{6,134},{7,135},{8... | collective-permute-start | bytes 245768 | tf_op jit(solution)/shard_map/ppermute | solution.py:50
  64.1 14.2 %collective-permute-done.5 = bf16[4,80,512]{2,1,0:T(8,128)(2,1)S(1)} collective-permute-done((bf16[4,80,512]{2,1,0:T(8,128)(2,1)S(1)}, bf16[4,80,512]{2,1,0:T(8,128)(2,1)S(1)}, u32[]{:S(2)}, u32[]{:S(2)}) %collective-permute-start.5) | collective-permute-done | bytes 327712 | tf_op jit(solution)/shard_map/ppermute | solution.py:50
  81.7 6.9 %collective-permute-done.7 = bf16[2,80,512]{2,1,0:T(8,128)(2,1)S(1)} collective-permute-done((bf16[2,80,512]{2,1,0:T(8,128)(2,1)S(1)}, bf16[2,80,512]{2,1,0:T(8,128)(2,1)S(1)}, u32[]{:S(2)}, u32[]{:S(2)}) %collective-permute-start.7) | collective-permute-done | bytes 163872 | tf_op jit(solution)/shard_map/ppermute | solution.py:50
  94.0 4.4 %collective-permute-start = (bf16[128,1408]{0,1:T(8,128)(2,1)S(1)}, bf16[128,1408]{0,1:T(8,128)(2,1)S(1)}, u32[]{:S(2)}, u32[]{:S(2)}) collective-permute-start(bf16[128,1408]{0,1:T(8,128)(2,1)S(1)} %pad_maximum_fusion.2), channel_id=1, source_target_pairs={{0,64},{1,65},{2,66},{3,67},{4,68},{5,69},{6,70},{7,71},{8,72},{9,... | collective-permute-start | bytes 1081352 | tf_op jit(solution)/shard_map/ppermute | solution.py:50
  98.7 16.3 %collective-permute-done = bf16[128,1408]{0,1:T(8,128)(2,1)S(1)} collective-permute-done((bf16[128,1408]{0,1:T(8,128)(2,1)S(1)}, bf16[128,1408]{0,1:T(8,128)(2,1)S(1)}, u32[]{:S(2)}, u32[]{:S(2)}) %collective-permute-start) | collective-permute-done | bytes 360480 | tf_op jit(solution)/shard_map/ppermute | solution.py:50
  117.9 3.6 %film.1.film_ref = bf16[560,512]{1,0:T(8,128)(2,1)S(1)} custom-call(s32[17]{0:T(128)S(1)} %stack.148.order_ref, bf16[16,256,80]{2,1,0:T(8,128)(2,1)S(1)} %bitcast.70, bf16[16,80,512]{2,1,0:T(8,128)(2,1)S(1)} %constant_dynamic-update-slice_fusion.mine_ref, bf16[16,80,512]{2,1,0:T(8,128)(2,1)} %collective-permute-done.9.sibling_ref, ...), custom_call_target="tpu_custom_call" | custom-call | flops 671088640 | bytes 4194304 | tf_op jit(solution)/shard_map/film/pallas_call | solution.py:127
  124.6 11.0 %collective-permute-done.10.film_ref = bf16[560,512]{1,0:T(8,128)(2,1)S(1)} collective-permute-done((bf16[560,512]{1,0:T(8,128)(2,1)S(1)}, bf16[560,512]{1,0:T(8,128)(2,1)S(1)}, u32[]{:S(2)}, u32[]{:S(2)}) %collective-permute-start.10) | collective-permute-done | bytes 573472 | tf_op jit(solution)/shard_map/ppermute | solution.py:50
  138.7 6.1 %collective-permute-done.11.film_ref = bf16[560,512]{1,0:T(8,128)(2,1)S(1)} collective-permute-done((bf16[560,512]{1,0:T(8,128)(2,1)S(1)}, bf16[560,512]{1,0:T(8,128)(2,1)S(1)}, u32[]{:S(2)}, u32[]{:S(2)}) %collective-permute-start.11) | collective-permute-done | bytes 573472 | tf_op jit(solution)/shard_map/ppermute | solution.py:50
  144.8 3.1 %collective-permute-start.12 = (bf16[560,512]{1,0:T(8,128)(2,1)S(1)}, bf16[560,512]{1,0:T(8,128)(2,1)S(1)}, u32[]{:S(2)}, u32[]{:S(2)}) collective-permute-start(bf16[560,512]{1,0:T(8,128)(2,1)S(1)} %collective-permute-done.11.film_ref), channel_id=1, source_target_pairs={{0,1},{1,2},{2,3},{3,0},{4,5},{5,6},{6,7},{7,4},{8,11},{9,8},{10,9... | collective-permute-start | bytes 1720328 | tf_op jit(solution)/shard_map/ppermute | solution.py:50
  151.0 3.1 %collective-permute-start.16 = (bf16[560,512]{1,0:T(8,128)(2,1)}, bf16[560,512]{1,0:T(8,128)(2,1)}, u32[]{:S(2)}, u32[]{:S(2)}) collective-permute-start(bf16[560,512]{1,0:T(8,128)(2,1)} %collective-permute-done.15.film_ref), channel_id=1, source_target_pairs={{0,1},{1,2},{2,3},{3,0},{4,5},{5,6},{6,7},{7,4},{8,11},{9,8},{10,9... | collective-permute-start | bytes 1720328 | tf_op jit(solution)/shard_map/ppermute | solution.py:50
  157.1 3.1 %collective-permute-start.13 = (bf16[560,512]{1,0:T(8,128)(2,1)S(1)}, bf16[560,512]{1,0:T(8,128)(2,1)}, u32[]{:S(2)}, u32[]{:S(2)}) collective-permute-start(bf16[560,512]{1,0:T(8,128)(2,1)S(1)} %collective-permute-done.12.film_ref), channel_id=1, source_target_pairs={{0,1},{1,2},{2,3},{3,0},{4,5},{5,6},{6,7},{7,4},{8,11},{9,8},{10,9... | collective-permute-start | bytes 1720328 | tf_op jit(solution)/shard_map/ppermute | solution.py:50
  162.2 4.3 %first.8.rest_0_ = bf16[8,1024,512]{2,1,0:T(8,128)(2,1)S(1)} custom-call(s32[1]{0:T(128)} %bitcast.39.place_ref, bf16[1024,48]{1,0:T(8,128)(2,1)S(1)} %pad.34.window_ref, bf16[560,512]{1,0:T(8,128)(2,1)S(1)} %film.1.film_ref), custom_call_target="tpu_custom_call" | custom-call | flops 50331648 | bytes 2097152 | tf_op jit(solution)/shard_map/first/pallas_call | solution.py:170
  166.6 5.4 %first.9.rest_0_ = bf16[8,1024,512]{2,1,0:T(8,128)(2,1)S(1)} custom-call(s32[1]{0:T(128)} %bitcast.38.place_ref, bf16[1024,48]{1,0:T(8,128)(2,1)S(1)} %pad.34.window_ref, bf16[560,512]{1,0:T(8,128)(2,1)} %collective-permute-done.14.film_ref, bf16[8,1024,512]{2,1,0:T(8,128)(2,1)S(1)} %first.8.rest_0_), custom_call_target="tpu_custom_call", output_to_operand_aliasing={{}: (3, {})} | custom-call | flops 50331648 | bytes 2097152 | tf_op jit(solution)/shard_map/first/pallas_call | solution.py:170
  172.0 4.3 %first.10.rest_0_ = bf16[8,1024,512]{2,1,0:T(8,128)(2,1)S(1)} custom-call(s32[1]{0:T(128)} %bitcast.37.place_ref, bf16[1024,48]{1,0:T(8,128)(2,1)S(1)} %pad.34.window_ref, bf16[560,512]{1,0:T(8,128)(2,1)S(1)} %collective-permute-done.10.film_ref, bf16[8,1024,512]{2,1,0:T(8,128)(2,1)S(1)} %first.9.rest_0_), custom_call_target="tpu_custom_call", output_to_operand_aliasing={{}: (3, {})} | custom-call | flops 50331648 | bytes 2097152 | tf_op jit(solution)/shard_map/first/pallas_call | solution.py:170
  176.3 5.4 %first.11.rest_0_ = bf16[8,1024,512]{2,1,0:T(8,128)(2,1)S(1)} custom-call(s32[1]{0:T(128)} %bitcast.36.place_ref, bf16[1024,48]{1,0:T(8,128)(2,1)S(1)} %pad.34.window_ref, bf16[560,512]{1,0:T(8,128)(2,1)} %collective-permute-done.15.film_ref, bf16[8,1024,512]{2,1,0:T(8,128)(2,1)S(1)} %first.10.rest_0_), custom_call_target="tpu_custom_call", output_to_operand_aliasing={{}: (3, {})} | custom-call | flops 50331648 | bytes 2097152 | tf_op jit(solution)/shard_map/first/pallas_call | solution.py:170
  181.7 4.3 %first.12.rest_0_ = bf16[8,1024,512]{2,1,0:T(8,128)(2,1)S(1)} custom-call(s32[1]{0:T(128)} %bitcast.35.place_ref, bf16[1024,48]{1,0:T(8,128)(2,1)S(1)} %pad.34.window_ref, bf16[560,512]{1,0:T(8,128)(2,1)S(1)} %collective-permute-done.11.film_ref, bf16[8,1024,512]{2,1,0:T(8,128)(2,1)S(1)} %first.11.rest_0_), custom_call_target="tpu_custom_call", output_to_operand_aliasing={{}: (3, {})} | custom-call | flops 50331648 | bytes 2097152 | tf_op jit(solution)/shard_map/first/pallas_call | solution.py:170
  186.0 5.4 %first.13.rest_0_ = bf16[8,1024,512]{2,1,0:T(8,128)(2,1)S(1)} custom-call(s32[1]{0:T(128)} %bitcast.34.place_ref, bf16[1024,48]{1,0:T(8,128)(2,1)S(1)} %pad.34.window_ref, bf16[560,512]{1,0:T(8,128)(2,1)} %collective-permute-done.16.film_ref, bf16[8,1024,512]{2,1,0:T(8,128)(2,1)S(1)} %first.12.rest_0_), custom_call_target="tpu_custom_call", output_to_operand_aliasing={{}: (3, {})} | custom-call | flops 50331648 | bytes 2097152 | tf_op jit(solution)/shard_map/first/pallas_call | solution.py:170
  191.4 4.3 %first.14.rest_0_ = bf16[8,1024,512]{2,1,0:T(8,128)(2,1)S(1)} custom-call(s32[1]{0:T(128)} %bitcast.33.place_ref, bf16[1024,48]{1,0:T(8,128)(2,1)S(1)} %pad.34.window_ref, bf16[560,512]{1,0:T(8,128)(2,1)S(1)} %collective-permute-done.12.film_ref, bf16[8,1024,512]{2,1,0:T(8,128)(2,1)S(1)} %first.13.rest_0_), custom_call_target="tpu_custom_call", output_to_operand_aliasing={{}: (3, {})} | custom-call | flops 50331648 | bytes 2097152 | tf_op jit(solution)/shard_map/first/pallas_call | solution.py:170
  195.7 5.4 %first.15.refs_1_ = bf16[8,1024,512]{2,1,0:T(8,128)(2,1)S(1)} custom-call(s32[1]{0:T(128)} %bitcast.6.place_ref, bf16[1024,48]{1,0:T(8,128)(2,1)S(1)} %pad.34.window_ref, bf16[560,512]{1,0:T(8,128)(2,1)} %collective-permute-done.13.film_ref, bf16[8,1024,512]{2,1,0:T(8,128)(2,1)S(1)} %first.14.rest_0_), custom_call_target="tpu_custom_call", output_to_operand_aliasing={{}: (3, {})} | custom-call | flops 50331648 | bytes 2097152 | tf_op jit(solution)/shard_map/first/pallas_call | solution.py:170
  201.1 3.3 %copy-done.1 = bf16[8,1024,512]{2,1,0:T(8,128)(2,1)} copy-done((bf16[8,1024,512]{2,1,0:T(8,128)(2,1)}, bf16[8,1024,512]{2,1,0:T(8,128)(2,1)S(1)}, u32[]{:S(2)}) %copy-start.1) | copy-done | bytes 8388632
  204.4 3.4 %copy-done.2 = bf16[8,1024,512]{2,1,0:T(8,128)(2,1)S(1)} copy-done((bf16[8,1024,512]{2,1,0:T(8,128)(2,1)S(1)}, bf16[8,1024,512]{2,1,0:T(8,128)(2,1)}, u32[]{:S(2)}) %copy-start.2) | copy-done | bytes 8388632
  212.5 3.4 %copy-done.3 = bf16[8,1024,512]{2,1,0:T(8,128)(2,1)S(1)} copy-done((bf16[8,1024,512]{2,1,0:T(8,128)(2,1)S(1)}, bf16[8,1024,512]{2,1,0:T(8,128)(2,1)}, u32[]{:S(2)}) %copy-start.3) | copy-done | bytes 8388632
  215.9 3.2 %copy-done.5 = bf16[24,5,128,256]{3,2,1,0:T(8,128)(2,1)S(1)} copy-done((bf16[24,5,128,256]{3,2,1,0:T(8,128)(2,1)S(1)}, bf16[24,5,128,256]{3,2,1,0:T(8,128)(2,1)}, u32[]{:S(2)}) %copy-start.5) | copy-done | bytes 7864344
  219.1 8.2 %mid.3 = (f32[1024,256]{1,0:T(8,128)S(1)}, f32[8,256]{1,0:T(8,128)S(1)}) custom-call(s32[6]{0:T(128)S(1)} %stack.130.refs_0_, bf16[8,1024,512]{2,1,0:T(8,128)(2,1)S(1)} %copy-done.3, bf16[8,3,5,128,256]{4,3,2,1,0:T(8,128)(2,1)S(1)} %bitcast.73, f32[1024,256]{1,0:T(8,128)S(1)} %mid.2.refs_3_), custom_call_target="tpu_custom_call" | custom-call | flops 5637144576 | bytes 15728640 | tf_op jit(solution)/shard_map/mid/pallas_call | solution.py:240
  232.8 4.6 %all-to-all-start = ((f32[16,32,128]{2,1,0:T(8,128)}), f32[16,32,128]{2,1,0:T(8,128)S(1)}, u32[]{:S(2)}, u32[]{:S(2)}) async-start(f32[16,32,128]{2,1,0:T(8,128)} %bitcast.53), calls=%async_computation | async-start | bytes 524288 | tf_op jit(solution)/shard_map/all_to_all | solution.py:392
  237.6 8.8 %all-to-all-done = f32[16,32,128]{2,1,0:T(8,128)S(1)} async-done(((f32[16,32,128]{2,1,0:T(8,128)}), f32[16,32,128]{2,1,0:T(8,128)S(1)}, u32[]{:S(2)}, u32[]{:S(2)}) %all-to-all-start) | async-done | bytes 262176 | tf_op jit(solution)/shard_map/all_to_all | solution.py:392
  (126 shorter events, 49.8 us)
Async XLA Ops:
  7.2 84.5 %copy-start = (bf16[1024,256]{1,0:T(8,128)(2,1)S(1)}, bf16[1024,256]{1,0:T(8,128)(2,1)}, u32[]{:S(2)}) copy-start(bf16[1024,256]{1,0:T(8,128)(2,1)} %param.19) | copy-start | bytes 1572868
  7.2 197.3 %all-gather.7.cloned.1.call-start = ((), (), s32[]{:S(2)}) async-start(), calls=%async_computation.2 | async-start | bytes 2949120 | tf_op jit(solution)/shard_map/all_gather | solution.py:320
  9.1 203.3 %all-gather.5.cloned.1.call-start = ((), (), s32[]{:S(2)}) async-start(), calls=%async_computation.1 | async-start | bytes 8847360 | tf_op jit(solution)/shard_map/all_gather | solution.py:322
  9.2 16.4 %collective-permute-start.17 = (bf16[5,128,256]{2,1,0:T(8,128)(2,1)S(1)}, bf16[5,128,256]{2,1,0:T(8,128)(2,1)S(1)}, u32[]{:S(2)}, u32[]{:S(2)}) collective-permute-start(bf16[5,128,256]{2,1,0:T(8,128)(2,1)S(1)} %get-tuple-element.15), channel_id=1, source_target_pairs={{0,64},{1,65},{2,66},{3,67},{4,68},{5,69},{6,70},{7,71},{8,72},{9,... | collective-permute-start | bytes 983048 | tf_op jit(solution)/shard_map/ppermute | solution.py:50
  13.1 26.7 %collective-permute-start.18 = (bf16[5,128,256]{2,1,0:T(8,128)(2,1)S(1)}, bf16[5,128,256]{2,1,0:T(8,128)(2,1)S(1)}, u32[]{:S(2)}, u32[]{:S(2)}) collective-permute-start(bf16[5,128,256]{2,1,0:T(8,128)(2,1)S(1)} %get-tuple-element.15), channel_id=1, source_target_pairs={{0,192},{1,193},{2,194},{3,195},{4,196},{5,197},{6,198},{7,199},{8... | collective-permute-start | bytes 983048 | tf_op jit(solution)/shard_map/ppermute | solution.py:50
  16.2 23.6 %collective-permute-start.19 = (bf16[5,128,256]{2,1,0:T(8,128)(2,1)}, bf16[5,128,256]{2,1,0:T(8,128)(2,1)S(1)}, u32[]{:S(2)}, u32[]{:S(2)}) collective-permute-start(bf16[5,128,256]{2,1,0:T(8,128)(2,1)} %get-tuple-element.16), channel_id=1, source_target_pairs={{0,128},{1,129},{2,130},{3,131},{4,132},{5,133},{6,134},{7,135},{8... | collective-permute-start | bytes 983048 | tf_op jit(solution)/shard_map/ppermute | solution.py:50
  41.1 2.2 collective-permute-start.1
  43.4 13.7 %collective-permute-start.2 = (bf16[80,512]{1,0:T(8,128)(2,1)S(1)}, bf16[80,512]{1,0:T(8,128)(2,1)S(1)}, u32[]{:S(2)}, u32[]{:S(2)}) collective-permute-start(bf16[80,512]{1,0:T(8,128)(2,1)S(1)} %maximum_select_fusion.2), channel_id=1, source_target_pairs={{0,64},{1,65},{2,66},{3,67},{4,68},{5,69},{6,70},{7,71},{8,72},{9,... | collective-permute-start | bytes 245768 | tf_op jit(solution)/shard_map/ppermute | solution.py:50
  53.2 6.5 %collective-permute-start.3 = (bf16[80,512]{1,0:T(8,128)(2,1)S(1)}, bf16[80,512]{1,0:T(8,128)(2,1)S(1)}, u32[]{:S(2)}, u32[]{:S(2)}) collective-permute-start(bf16[80,512]{1,0:T(8,128)(2,1)S(1)} %maximum_select_fusion.2), channel_id=1, source_target_pairs={{0,192},{1,193},{2,194},{3,195},{4,196},{5,197},{6,198},{7,199},{8... | collective-permute-start | bytes 245768 | tf_op jit(solution)/shard_map/ppermute | solution.py:50
  53.2 7.9 %collective-permute-start.4 = (bf16[80,512]{1,0:T(8,128)(2,1)S(1)}, bf16[80,512]{1,0:T(8,128)(2,1)S(1)}, u32[]{:S(2)}, u32[]{:S(2)}) collective-permute-start(bf16[80,512]{1,0:T(8,128)(2,1)S(1)} %maximum_select_fusion.2), channel_id=1, source_target_pairs={{0,128},{1,129},{2,130},{3,131},{4,132},{5,133},{6,134},{7,135},{8... | collective-permute-start | bytes 245768 | tf_op jit(solution)/shard_map/ppermute | solution.py:50
  61.2 17.2 %collective-permute-start.5 = (bf16[4,80,512]{2,1,0:T(8,128)(2,1)S(1)}, bf16[4,80,512]{2,1,0:T(8,128)(2,1)S(1)}, u32[]{:S(2)}, u32[]{:S(2)}) collective-permute-start(bf16[4,80,512]{2,1,0:T(8,128)(2,1)S(1)} %pad_maximum_fusion.3), channel_id=1, source_target_pairs={{0,16},{1,17},{2,18},{3,19},{4,20},{5,21},{6,22},{7,23},{8,24},{9,... | collective-permute-start | bytes 983048 | tf_op jit(solution)/shard_map/ppermute | solution.py:50
  62.6 16.2 %collective-permute-start.6 = (bf16[4,80,512]{2,1,0:T(8,128)(2,1)S(1)}, bf16[4,80,512]{2,1,0:T(8,128)(2,1)S(1)}, u32[]{:S(2)}, u32[]{:S(2)}) collective-permute-start(bf16[4,80,512]{2,1,0:T(8,128)(2,1)S(1)} %pad_maximum_fusion.3), channel_id=1, source_target_pairs={{0,48},{1,49},{2,50},{3,51},{4,52},{5,53},{6,54},{7,55},{8,56},{9,... | collective-permute-start | bytes 983048 | tf_op jit(solution)/shard_map/ppermute | solution.py:50
  78.4 10.2 %collective-permute-start.7 = (bf16[2,80,512]{2,1,0:T(8,128)(2,1)S(1)}, bf16[2,80,512]{2,1,0:T(8,128)(2,1)S(1)}, u32[]{:S(2)}, u32[]{:S(2)}) collective-permute-start(bf16[2,80,512]{2,1,0:T(8,128)(2,1)S(1)} %slice.38), channel_id=1, source_target_pairs={{0,16},{1,17},{2,18},{3,19},{4,20},{5,21},{6,22},{7,23},{8,24},{9,... | collective-permute-start | bytes 491528 | tf_op jit(solution)/shard_map/ppermute | solution.py:50
  78.8 9.8 %collective-permute-start.8 = (bf16[2,80,512]{2,1,0:T(8,128)(2,1)S(1)}, bf16[2,80,512]{2,1,0:T(8,128)(2,1)S(1)}, u32[]{:S(2)}, u32[]{:S(2)}) collective-permute-start(bf16[2,80,512]{2,1,0:T(8,128)(2,1)S(1)} %slice.39), channel_id=1, source_target_pairs={{0,48},{1,49},{2,50},{3,51},{4,52},{5,53},{6,54},{7,55},{8,56},{9,... | collective-permute-start | bytes 491528 | tf_op jit(solution)/shard_map/ppermute | solution.py:50
  88.6 29.2 %collective-permute-start.9 = (bf16[16,80,512]{2,1,0:T(8,128)(2,1)S(1)}, bf16[16,80,512]{2,1,0:T(8,128)(2,1)}, u32[]{:S(2)}, u32[]{:S(2)}) collective-permute-start(bf16[16,80,512]{2,1,0:T(8,128)(2,1)S(1)} %constant_dynamic-update-slice_fusion.mine_ref), channel_id=1, source_target_pairs={{0,8},{1,9},{2,10},{3,11},{4,12},{5,13},{6,14},{7,15},{8,0},{9,1},... | collective-permute-start | bytes 3932168 | tf_op jit(solution)/shard_map/ppermute | solution.py:50
  94.0 21.0 %collective-permute-start = (bf16[128,1408]{0,1:T(8,128)(2,1)S(1)}, bf16[128,1408]{0,1:T(8,128)(2,1)S(1)}, u32[]{:S(2)}, u32[]{:S(2)}) collective-permute-start(bf16[128,1408]{0,1:T(8,128)(2,1)S(1)} %pad_maximum_fusion.2), channel_id=1, source_target_pairs={{0,64},{1,65},{2,66},{3,67},{4,68},{5,69},{6,70},{7,71},{8,72},{9,... | collective-permute-start | bytes 1081352 | tf_op jit(solution)/shard_map/ppermute | solution.py:50
  117.9 30.1 %copy-start.12 = (bf16[512,7]{0,1:T(8,128)(2,1)S(1)}, bf16[512,7]{0,1:T(8,128)(2,1)}, u32[]{:S(2)}) copy-start(bf16[512,7]{0,1:T(8,128)(2,1)} %param.24) | copy-start | bytes 21508
  117.9 42.4 %slice-start = ((bf16[256,1408]{0,1:T(8,128)(2,1)}), bf16[256,28]{0,1:T(8,128)(2,1)S(1)}, s32[]{:S(2)}) async-start(bf16[256,1408]{0,1:T(8,128)(2,1)} %copy-done.6), calls=%async_computation.3 | async-start | bytes 32768 | tf_op jit(solution)/shard_map/slice | solution.py:350
  121.5 14.1 %collective-permute-start.10 = (bf16[560,512]{1,0:T(8,128)(2,1)S(1)}, bf16[560,512]{1,0:T(8,128)(2,1)S(1)}, u32[]{:S(2)}, u32[]{:S(2)}) collective-permute-start(bf16[560,512]{1,0:T(8,128)(2,1)S(1)} %film.1.film_ref), channel_id=1, source_target_pairs={{0,4},{1,5},{2,6},{3,7},{4,0},{5,1},{6,2},{7,3},{8,12},{9,13},{10,... | collective-permute-start | bytes 1720328 | tf_op jit(solution)/shard_map/ppermute | solution.py:50
  122.1 16.0 %collective-permute-start.14 = (bf16[560,512]{1,0:T(8,128)(2,1)S(1)}, bf16[560,512]{1,0:T(8,128)(2,1)}, u32[]{:S(2)}, u32[]{:S(2)}) collective-permute-start(bf16[560,512]{1,0:T(8,128)(2,1)S(1)} %film.1.film_ref), channel_id=1, source_target_pairs={{0,1},{1,2},{2,3},{3,0},{4,5},{5,6},{6,7},{7,4},{8,11},{9,8},{10,9... | collective-permute-start | bytes 1720328 | tf_op jit(solution)/shard_map/ppermute | solution.py:50
  135.6 9.1 %collective-permute-start.11 = (bf16[560,512]{1,0:T(8,128)(2,1)S(1)}, bf16[560,512]{1,0:T(8,128)(2,1)S(1)}, u32[]{:S(2)}, u32[]{:S(2)}) collective-permute-start(bf16[560,512]{1,0:T(8,128)(2,1)S(1)} %collective-permute-done.10.film_ref), channel_id=1, source_target_pairs={{0,1},{1,2},{2,3},{3,0},{4,5},{5,6},{6,7},{7,4},{8,11},{9,8},{10,9... | collective-permute-start | bytes 1720328 | tf_op jit(solution)/shard_map/ppermute | solution.py:50
  138.1 12.9 %collective-permute-start.15 = (bf16[560,512]{1,0:T(8,128)(2,1)}, bf16[560,512]{1,0:T(8,128)(2,1)}, u32[]{:S(2)}, u32[]{:S(2)}) collective-permute-start(bf16[560,512]{1,0:T(8,128)(2,1)} %collective-permute-done.14.film_ref), channel_id=1, source_target_pairs={{0,1},{1,2},{2,3},{3,0},{4,5},{5,6},{6,7},{7,4},{8,11},{9,8},{10,9... | collective-permute-start | bytes 1720328 | tf_op jit(solution)/shard_map/ppermute | solution.py:50
  144.8 12.3 %collective-permute-start.12 = (bf16[560,512]{1,0:T(8,128)(2,1)S(1)}, bf16[560,512]{1,0:T(8,128)(2,1)S(1)}, u32[]{:S(2)}, u32[]{:S(2)}) collective-permute-start(bf16[560,512]{1,0:T(8,128)(2,1)S(1)} %collective-permute-done.11.film_ref), channel_id=1, source_target_pairs={{0,1},{1,2},{2,3},{3,0},{4,5},{5,6},{6,7},{7,4},{8,11},{9,8},{10,9... | collective-permute-start | bytes 1720328 | tf_op jit(solution)/shard_map/ppermute | solution.py:50
  151.0 35.0 %collective-permute-start.16 = (bf16[560,512]{1,0:T(8,128)(2,1)}, bf16[560,512]{1,0:T(8,128)(2,1)}, u32[]{:S(2)}, u32[]{:S(2)}) collective-permute-start(bf16[560,512]{1,0:T(8,128)(2,1)} %collective-permute-done.15.film_ref), channel_id=1, source_target_pairs={{0,1},{1,2},{2,3},{3,0},{4,5},{5,6},{6,7},{7,4},{8,11},{9,8},{10,9... | collective-permute-start | bytes 1720328 | tf_op jit(solution)/shard_map/ppermute | solution.py:50
  157.1 38.7 %collective-permute-start.13 = (bf16[560,512]{1,0:T(8,128)(2,1)S(1)}, bf16[560,512]{1,0:T(8,128)(2,1)}, u32[]{:S(2)}, u32[]{:S(2)}) collective-permute-start(bf16[560,512]{1,0:T(8,128)(2,1)S(1)} %collective-permute-done.12.film_ref), channel_id=1, source_target_pairs={{0,1},{1,2},{2,3},{3,0},{4,5},{5,6},{6,7},{7,4},{8,11},{9,8},{10,9... | collective-permute-start | bytes 1720328 | tf_op jit(solution)/shard_map/ppermute | solution.py:50
  219.1 11.0 %copy-start.13 = (bf16[7,512]{1,0:T(8,128)(2,1)S(1)}, bf16[7,512]{1,0:T(8,128)(2,1)}, u32[]{:S(2)}) copy-start(bf16[7,512]{1,0:T(8,128)(2,1)} %param.22) | copy-start | bytes 21508
  219.1 11.0 %copy-start.18 = (f32[512]{0:T(512)S(1)}, f32[512]{0:T(512)}, u32[]{:S(2)}) copy-start(f32[512]{0:T(512)} %param.26) | copy-start | bytes 6148
  227.4 10.1 %copy-start.16 = (f32[100]{0:T(128)S(1)}, f32[100]{0:T(128)}, u32[]{:S(2)}) copy-start(f32[100]{0:T(128)} %constant.198.clone) | copy-start | bytes 1204
  227.4 10.1 %copy-start.17 = (s32[128]{0:T(128)S(1)}, s32[128]{0:T(128)}, u32[]{:S(2)}) copy-start(s32[128]{0:T(128)} %get-tuple-element.36) | copy-start | bytes 1540
  227.4 3.7 %collective-permute-start.20 = (f32[8,256]{1,0:T(8,128)S(1)}, f32[8,256]{1,0:T(8,128)S(1)}, u32[]{:S(2)}, u32[]{:S(2)}) collective-permute-start(f32[8,256]{1,0:T(8,128)S(1)} %get-tuple-element.5.own_ref), channel_id=1, source_target_pairs={{0,64},{1,65},{2,66},{3,67},{4,68},{5,69},{6,70},{7,71},{8,72},{9,... | collective-permute-start | bytes 24584 | tf_op jit(solution)/shard_map/ppermute | solution.py:50
  230.1 16.3 %copy-start.11 = (f32[128,28]{0,1:T(8,128)S(1)}, f32[128,28]{0,1:T(8,128)}, u32[]{:S(2)}) copy-start(f32[128,28]{0,1:T(8,128)} %param.16) | copy-start | bytes 43012
  232.8 13.6 %all-to-all-start = ((f32[16,32,128]{2,1,0:T(8,128)}), f32[16,32,128]{2,1,0:T(8,128)S(1)}, u32[]{:S(2)}, u32[]{:S(2)}) async-start(f32[16,32,128]{2,1,0:T(8,128)} %bitcast.53), calls=%async_computation | async-start | bytes 524288 | tf_op jit(solution)/shard_map/all_to_all | solution.py:392
  (12 other events, 33.9 us)
Sparse Core Ops, SparseCore 0:
  9.8 32.9 all-gather.6
  44.6 63.8 all-gather.4

commit v2 on v1

--- a/solution.py
+++ b/solution.py
@@ -58,6 +58,7 @@
 y_down = mover(lambda zh, y, core, zl, x: (zh, y - 1, core, zl, x))
 cores = mover(lambda zh, y, core, zl, x: (zh, y, 1 - core, zl, x))
 zl_swap = mover(lambda zh, y, core, zl, x: (zh, y, core, 1 - zl, x))
+y_ring = mover(lambda zh, y, core, zl, x: (zh, y + 1 - 2 * core, core, zl, x))
 x_ring = mover(lambda zh, y, core, zl, x: (zh, y, core, zl, x + 1 - 2 * core))
 
 
@@ -80,7 +81,14 @@
 def mish_by_exp(value):
     u = jnp.exp(jnp.minimum(value, 20.0))
     w = u * (u + 2.0)
-    return value * (w / (w + 2.0))
+    below = w + 2.0
+    inv = pl.reciprocal(below, approx=True)
+    inv = inv * (2.0 - below * inv)
+    return value * (w * inv)
+
+
+def tie(*arrays):
+    return lax.optimization_barrier(arrays)
 
 
 def sinusoid(steps):
@@ -138,7 +146,7 @@
     )(order, cond_blocks, mine, sibling, small)
 
 
-def first_kernel(place_ref, window_ref, film_ref, *rest):
+def first_kernel(slot, window_ref, film_ref, *rest):
     out_ref, hidden_ref = rest[-2:]
     hidden_ref[...] = jnp.dot(
         window_ref[...], film_ref[2 * PAIR :, :], preferred_element_type=f32
@@ -147,74 +155,111 @@
         film_ref[2 * PAIR + 35 : 2 * PAIR + 36, :].astype(f32)
         + film_ref[2 * PAIR + 36 : 2 * PAIR + 37, :].astype(f32)
     )
-    some = 16
+
+    def lanes(value):
+        return sum(value[:, c : c + 128] for c in range(0, WIDE, 128))
+
+    some, few = 64, 16
 
     @pl.loop(0, PAIR // some)
     def _(step):
         at = [pl.multiple_of(p * PAIR + step * some, some) for p in range(HORIZON)]
-        hidden = [hidden_ref[pl.ds(a, some), :] for a in at]
-        mean = jnp.sum(sum(hidden), axis=1, keepdims=True) * (1.0 / (HORIZON * WIDE))
-        off = [h - mean for h in hidden]
-        var = jnp.sum(sum(o * o for o in off), axis=1, keepdims=True) * (1.0 / (HORIZON * WIDE))
+        total = sum(lanes(hidden_ref[pl.ds(a, some), :]) for a in at)
+        mean = jnp.sum(total, axis=1, keepdims=True) * (1.0 / (HORIZON * WIDE))
+        total = sum(lanes((hidden_ref[pl.ds(a, some), :] - mean) ** 2) for a in at)
+        var = jnp.sum(total, axis=1, keepdims=True) * (1.0 / (HORIZON * WIDE))
         inv = lax.rsqrt(var + 1e-05)
-        scale = film_ref[pl.ds(at[0], some), :].astype(f32)
-        shift = film_ref[pl.ds(at[1], some), :].astype(f32)
-        for a, o in zip(at, off):
-            out_ref[0, pl.ds(a, some), :] = (
-                scale * mish_by_exp(o * inv * gain) + shift
-            ).astype(bf16)
-
-
-def first_of(place, window, film, before):
+        for r in range(0, some, few):
+            base = step * some + r
+            scale = film_ref[pl.ds(pl.multiple_of(base, few), few), :].astype(f32)
+            shift = film_ref[pl.ds(pl.multiple_of(PAIR + base, few), few), :].astype(f32)
+            for p in range(HORIZON):
+                a = pl.multiple_of(p * PAIR + base, few)
+                normed = (hidden_ref[pl.ds(a, few), :] - mean[r : r + few]) * inv[r : r + few]
+                out_ref[0, pl.ds(a, few), :] = (
+                    scale * mish_by_exp(normed * gain) + shift
+                ).astype(bf16)
+
+
+def first_of(slot, window, film, before):
     more = [] if before is None else [before]
     return pl.pallas_call(
-        first_kernel,
+        lambda *refs: first_kernel(slot, *refs),
         out_shape=jax.ShapeDtypeStruct((8, ROWS, WIDE), bf16),
-        grid_spec=pltpu.PrefetchScalarGridSpec(
-            num_scalar_prefetch=1,
-            grid=(1,),
-            in_specs=[
-                pl.BlockSpec((ROWS, WIN), lambda i, place: (0, 0)),
-                pl.BlockSpec((FILM_ROWS, WIDE), lambda i, place: (0, 0)),
-            ]
-            + [pl.BlockSpec(memory_space=pl.ANY)] * len(more),
-            out_specs=pl.BlockSpec((1, ROWS, WIDE), lambda i, place: (place[0], 0, 0)),
-            scratch_shapes=[pltpu.VMEM((ROWS, WIDE), f32)],
-        ),
-        input_output_aliases={3: 0} if more else {},
-        compiler_params=params(24),
+        grid=(1,),
+        in_specs=[
+            pl.BlockSpec((ROWS, WIN), lambda i: (0, 0)),
+            pl.BlockSpec((FILM_ROWS, WIDE), lambda i: (0, 0)),
+        ]
+        + [pl.BlockSpec(memory_space=pl.ANY)] * len(more),
+        out_specs=pl.BlockSpec((1, ROWS, WIDE), lambda i: (slot, 0, 0)),
+        scratch_shapes=[pltpu.VMEM((ROWS, WIDE), f32)],
+        input_output_aliases={2: 0} if more else {},
+        compiler_params=params(56),
         cost_estimate=pl.CostEstimate(
             flops=2 * ROWS * WIN * WIDE, bytes_accessed=2 * 2**20, transcendentals=ROWS * WIDE
         ),
         name="first",
-    )(place, window, film, *more)
-
-
-def mid_kernel(stats, place_ref, act_ref, weight_ref, *rest):
+    )(window, film, *more)
+
+
+def mid_kernel(count, stats, place_ref, act_ref, own_ref, near_ref, mine_ref, theirs_ref, *rest):
     rest = list(rest)
+    sems, held = rest.pop(), rest.pop()
     stats_ref = rest.pop() if stats else None
     out_ref = rest.pop()
-    j, q = pl.program_id(0), pl.program_id(1)
-
-    @pl.when(jnp.logical_and(j == 0, q == 0))
+    i = pl.program_id(0)
+    zh, y, core = place_ref[0], place_ref[1], place_ref[2]
+
+    def fetch(step, slot):
+        block = place_ref[3 + step]
+        q, apart = block % 2, (block // 2 + 4 - zh) % 4
+        into, sem = held.at[slot], sems.at[slot]
+
+        @pl.when(apart == 0)
+        def _():
+            pltpu.make_async_copy(own_ref.at[pl.ds(4 * q, 4)], into, sem).start()
+
+        for way, side in ((3, 0), (1, 1)):
+
+            @pl.when(apart == way)
+            def _():
+                pltpu.make_async_copy(near_ref.at[pl.ds(4 * q, 4), side], into, sem).start()
+
+        @pl.when(apart == 2)
+        def _():
+            for odd in range(2):
+                for ref, its in ((mine_ref, core), (theirs_ref, 1 - core)):
+                    steps = (1 - 2 * its) * (y - 2 * q - odd)
+                    source = ref.at[(steps + 8) % 4]
+                    pltpu.make_async_copy(source, into.at[2 * odd + its], sem).start()
+
+    @pl.when(i == 0)
+    def _():
+        fetch(0, 0)
+
+    @pl.when(i + 1 < count)
+    def _():
+        fetch(i + 1, (i + 1) % 2)
+
+    @pl.when(i == 0)
     def _():
         out_ref[...] = rest[0][...] if rest else jnp.zeros_like(out_ref)
 
-    for h in range(HORIZON):
-        total = out_ref[h * PAIR : (h + 1) * PAIR, :]
-        for p in range(HORIZON):
-            k = p - h + 2
-            if 0 <= k < TAPS:
-                total += jnp.dot(
-                    act_ref[0, p * PAIR : (p + 1) * PAIR, :],
-                    weight_ref[:, 0, k].reshape(WIDE, HALF),
-                    preferred_element_type=f32,
-                )
-        out_ref[h * PAIR : (h + 1) * PAIR, :] = total
+    slot = i % 2
+    pltpu.make_async_copy(own_ref.at[pl.ds(0, 4)], held.at[slot], sems.at[slot]).wait()
+    for k in (2, 1, 3, 0, 4):
+        low, high = max(0, k - 2), min(HORIZON, HORIZON + k - 2)
+        rows = jnp.dot(
+            act_ref[0, low * PAIR : high * PAIR, :],
+            held[slot, :, k].reshape(WIDE, HALF),
+            preferred_element_type=f32,
+        )
+        out_ref[(low - k + 2) * PAIR : (high - k + 2) * PAIR, :] += rows
 
     if stats:
 
-        @pl.when(jnp.logical_and(j == pl.num_programs(0) - 1, q == 1))
+        @pl.when(i == count - 1)
         def _():
             parts = [out_ref[h * PAIR : (h + 1) * PAIR, :] for h in range(HORIZON)]
             mean = jnp.sum(sum(parts), axis=1, keepdims=True) * (1.0 / (HORIZON * HALF))
@@ -224,42 +269,37 @@
             stats_ref[...] = both.T[:8, :]
 
 
-def mid_of(place, acts, weights, before, stats):
-    pieces = weights.shape[1]
+def mid_of(place, start, count, acts, weights, before, stats):
     more = [] if before is None else [before]
-    whole = pl.BlockSpec((ROWS, HALF), lambda j, q, place: (0, 0))
+    whole = pl.BlockSpec((ROWS, HALF), lambda i: (0, 0))
     out_shape = [jax.ShapeDtypeStruct((ROWS, HALF), f32)]
     out_specs = [whole]
     if stats:
         out_shape.append(jax.ShapeDtypeStruct((8, PAIR), f32))
-        out_specs.append(pl.BlockSpec((8, PAIR), lambda j, q, place: (0, 0)))
-
-    def kernel(*refs):
-        mid_kernel(stats, *refs)
-
+        out_specs.append(pl.BlockSpec((8, PAIR), lambda i: (0, 0)))
     return pl.pallas_call(
-        kernel,
+        lambda *refs: mid_kernel(count, stats, *refs),
         out_shape=out_shape,
-        grid_spec=pltpu.PrefetchScalarGridSpec(
-            num_scalar_prefetch=1,
-            grid=(pieces, 2),
-            in_specs=[
-                pl.BlockSpec((1, ROWS, WIDE), lambda j, q, place: (place[2 * j + q], 0, 0)),
-                pl.BlockSpec(
-                    (4, 1, TAPS, OWN, HALF), lambda j, q, place: (q, j, 0, 0, 0)
-                ),
-            ]
-            + [whole] * len(more),
-            out_specs=out_specs,
-        ),
-        compiler_params=params(28),
+        grid=(count,),
+        in_specs=[
+            pl.BlockSpec(memory_space=pltpu.SMEM),
+            pl.BlockSpec((1, ROWS, WIDE), lambda i: (start + i, 0, 0)),
+        ]
+        + [pl.BlockSpec(memory_space=pl.ANY)] * 4
+        + [whole] * len(more),
+        out_specs=out_specs,
+        scratch_shapes=[
+            pltpu.VMEM((2, 4, TAPS, OWN, HALF), bf16),
+            pltpu.SemaphoreType.DMA((2,)),
+        ],
+        compiler_params=params(56),
         cost_estimate=pl.CostEstimate(
-            flops=2 * pieces * 2 * 14 * PAIR * WIDE * HALF,
-            bytes_accessed=pieces * 5 * 2**20,
+            flops=2 * count * 14 * PAIR * WIDE * HALF,
+            bytes_accessed=count * 5 * 2**19,
             transcendentals=0,
         ),
         name="mid",
-    )(place, acts, weights, *more)
+    )(place, acts, *weights, *more)
 
 
 def last_kernel(conv_ref, own_ref, other_ref, gain_ref, window_ref, res_ref, out_w_ref, eps_ref):
@@ -315,26 +355,20 @@
     zq, zp, y, core, zl, x = (lax.axis_index(a) for a in AXES)
     zh = 2 * zq + zp
 
-    keep = lax.dynamic_slice_in_dim(conv_mid_w, zp * HALF, HALF, 2)
-    give = lax.dynamic_slice_in_dim(conv_mid_w, (1 - zp) * HALF, HALF, 2)
-    w_own = lax.all_gather(keep[None], ("y", "core"), axis=0, tiled=False)
-    w_rest = jnp.stack([z_up(give), z_down(give), z_two(keep)])
-    w_rest = lax.all_gather(w_rest, ("y", "core"), axis=0, tiled=False)
-
     stay = lax.dynamic_index_in_dim(film_weight, core, 1, keepdims=False)
     go = lax.dynamic_index_in_dim(film_weight, 1 - core, 1, keepdims=False)
     come = cores(go)
+
+    keep = lax.dynamic_slice_in_dim(conv_mid_w, zp * HALF, HALF, 2)
+    give = lax.dynamic_slice_in_dim(conv_mid_w, (1 - zp) * HALF, HALF, 2)
+    w_own = lax.all_gather(keep, ("y", "core"), axis=0, tiled=False)
+
     chip = jnp.where(
         core == 0, jnp.concatenate([stay, come]), jnp.concatenate([come, stay])
     )
+    chip, give = tie(chip, give)
     line = jnp.stack([chip, z_up(chip), z_down(chip), z_two(chip)])
-    from_down, from_up = y_up(line), y_down(line)
-    far_a, far_b = y_up(from_down[:2]), y_down(from_up[2:])
-    mine = jnp.concatenate([line, from_down, from_up, far_a, far_b])
-    sibling = cores(mine)
-    dz = (0, -1, 1, 2)
-    order = [((zh + dz[r % 4]) % 4) * 4 + (y + dy) % 4 for dy in (0, -1, 1, 2) for r in range(4)]
-    order = jnp.stack(order + [core]).astype(jnp.int32)
+    w_up, w_down = z_up(give), z_down(give)
 
     sample_b = noisy_sample.astype(bf16)
     sinus = sinusoid(timestep).astype(bf16)
@@ -343,6 +377,15 @@
     cond = mish(jnp.concatenate([step_feat, obs_feat.astype(f32)], axis=1)).astype(bf16)
     packed = jnp.concatenate([cond, jnp.pad(sample_b, ((0, 0), (0, 100)))], axis=1)
     partner = z_pair(packed)
+
+    from_down, from_up = y_up(line), y_down(line)
+    from_down, from_up, partner, w_up, w_down, keep = tie(
+        from_down, from_up, partner, w_up, w_down, keep
+    )
+    far_a, far_b = y_up(from_down[:2]), y_down(from_up[2:])
+    w_near = lax.all_gather(jnp.stack([w_up, w_down]), ("y", "core"), axis=0, tiled=False)
+    w_far = z_two(keep)
+
     both = jnp.where(
         zp == 0, jnp.concatenate([packed, partner]), jnp.concatenate([partner, packed])
     )
@@ -350,7 +393,6 @@
     samples = jnp.pad(both[:, COND : COND + 28], ((0, 0), (14, 14)))
     window = jnp.concatenate([samples[:, 7 * p : 7 * p + 35] for p in range(HORIZON)])
     window = jnp.pad(window, ((0, 0), (0, WIN - 35)))
-
     coarse = lax.reduce_precision(gain_one, 8, 7)
     small = jnp.concatenate(
         [
@@ -360,25 +402,55 @@
             jnp.zeros((WIN - 37, WIDE), bf16),
         ]
     )
+
+    mine = jnp.concatenate([line, from_down, from_up, far_a, far_b])
+    mine, cond_blocks, window, small = tie(mine, cond_blocks, window, small)
+    sibling = cores(mine)
+    dz = (0, -1, 1, 2)
+    order = [((zh + dz[r % 4]) % 4) * 4 + (y + dy) % 4 for dy in (0, -1, 1, 2) for r in range(4)]
+    order = jnp.stack(order + [core]).astype(jnp.int32)
     film = film_of(order, cond_blocks, mine, sibling, small)
 
-    a, b = [film], [zl_swap(film)]
-    for _ in range(3):
-        a.append(x_ring(a[-1]))
-        b.append(x_ring(b[-1]))
-    acts = None
-    for side, step in ((0, 0), (0, 1), (1, 0), (0, 2), (1, 1), (0, 3), (1, 2), (1, 3)):
-        owner = (x + step * (2 * core - 1)) % 4
-        block = jnp.where(side == 0, zl, 1 - zl) * 4 + owner
-        acts = first_of(
-            block.reshape(1).astype(jnp.int32), window, (a if side == 0 else b)[step], acts
-        )
-
-    def blocks(*shifts):
-        return jnp.stack([((zh + s) % 4) * 2 + q for s in shifts for q in range(2)]).astype(jnp.int32)
-
-    [conv] = mid_of(blocks(0), acts, w_own, None, False)
-    conv, stats = mid_of(blocks(-1, 1, 2), acts, w_rest, conv, True)
+    film, w_far = tie(film, w_far)
+    a_one, b_own, far_one = x_ring(film), zl_swap(film), y_ring(w_far)
+    acts = first_of(0, window, film, None)
+    a_one, acts = tie(a_one, acts)
+    a_two = x_ring(a_one)
+    b_own, acts = tie(b_own, acts)
+    b_one = x_ring(b_own)
+    acts = first_of(1, window, a_one, acts)
+    far_one, acts = tie(far_one, acts)
+    far_two = y_ring(far_one)
+    acts = first_of(2, window, b_own, acts)
+    a_two, acts = tie(a_two, acts)
+    a_three = x_ring(a_two)
+    acts = first_of(3, window, a_two, acts)
+    b_one, acts = tie(b_one, acts)
+    b_two = x_ring(b_one)
+    far_two, acts = tie(far_two, acts)
+    far_three = y_ring(far_two)
+    acts = first_of(4, window, b_one, acts)
+    acts = first_of(5, window, a_three, acts)
+    b_two, acts = tie(b_two, acts)
+    b_three = x_ring(b_two)
+    far_three, acts = tie(far_three, acts)
+    far_mine = jnp.stack([w_far, far_one, far_two, far_three])
+    far_theirs = cores(far_mine)
+    acts = first_of(6, window, b_two, acts)
+
+    side = (0, 0, 1, 0, 1, 0, 1, 1)
+    step = (0, 1, 0, 2, 1, 3, 2, 3)
+    slots = [
+        (zl if b == 0 else 1 - zl) * 4 + (x + s * (2 * core - 1)) % 4 for b, s in zip(side, step)
+    ]
+    where = [zh, y, core]
+    early = jnp.stack(where + slots[:7]).astype(jnp.int32)
+    late = jnp.stack(where + slots[7:]).astype(jnp.int32)
+    weights = (w_own, w_near, far_mine, far_theirs)
+    [conv] = mid_of(early, 0, 7, acts, weights, None, False)
+    acts, conv = tie(acts, conv)
+    acts = first_of(7, window, b_three, acts)
+    conv, stats = mid_of(late, 7, 1, acts, weights, conv, True)
     other = z_pair(stats)
 
     out_h = lax.dynamic_slice_in_dim(out_w, zp * HALF, HALF, 0).T

time: 258 us -> 206 us (0.80)
  waiting for transfers between devices: 94 us -> 63 us
  starting transfers between devices: 62.1 us -> 42.8 us
  local copies, waits for them, and re-layouts: 23.1 us -> 16.8 us
  Pallas kernels: 54.5 us -> 59.5 us
    ppermute x21 -> x25, waiting for transfers between devices: 85.2 us -> 53.5 us  [mover(): return lambda array: lax.ppermute(array, AXES, pairs)]
    ppermute x21 -> x25, starting transfers between devices: 57.5 us -> 38.1 us  [mover(): return lambda array: lax.ppermute(array, AXES, pairs)]
    unnamed x47 -> x72, local copies, waits for them, and re-layouts: 15.4 us -> 6.37 us
    pallas_call x10, Pallas kernels: 49.9 us -> 54.8 us  [the longest x8 36.7 us: first_of(): pl.pallas_call(lambda *refs: first_kernel(slot, *refs), out_shape=jax.Sha...]
  transfers between devices with their start and end apart: 24 -> 28, of which waited for: 14 -> 9; matrix products, arithmetic and copies ran while one was open for 4% -> 7% of each run, Pallas kernels for 18% -> 24%
where the time goes in v2:
time: 206 us; the launch traced here: 204 us
  waiting for transfers between devices  63 us (31%)
  Pallas kernels  59.5 us (29%)
  starting transfers between devices  42.8 us (21%)
  local copies, waits for them, and re-layouts  16.8 us (8%)
  between operations  14.7 us (7%)
  other arithmetic  6.02 us (3%)
    ppermute x25, waiting for transfers between devices, mover(): return lambda array: lax.ppermute(array, AXES, pairs)  53.5 us
    ppermute x25, starting transfers between devices, mover(): return lambda array: lax.ppermute(array, AXES, pairs)  38.1 us
    pallas_call x8, Pallas kernels, first_of(): pl.pallas_call(lambda *refs: first_kernel(slot, *refs), out_shape=jax.Sha...  36.7 us
    pallas_call x2, Pallas kernels, mid_of(): pl.pallas_call(lambda *refs: mid_kernel(count, stats, *refs), out_shape=o...  18.1 us
    all_to_all x1, waiting for transfers between devices, body(): lax.all_to_all(sent, ('zp', 'zl', 'x'), split_axis=0, concat_axis=0, tile...  9.42 us
    unnamed x72, local copies, waits for them, and re-layouts  6.37 us
    all_to_all x1, starting transfers between devices, body(): lax.all_to_all(sent, ('zp', 'zl', 'x'), split_axis=0, concat_axis=0, tile...  4.57 us
  transfers between devices with their start and end apart: 28, of which 9 were waited for; matrix products, arithmetic and copies ran while one was open for 7% of the time, Pallas kernels for 24%

profile of v2, /device:TPU:1, one launch (start us, length us, event | category | flops | bytes accessed | tf_op | source)
XLA Modules:
  0.0 203.5 jit_solution(4889549507006278896)
XLA Ops:
  7.3 1.9 constant_dynamic-slice_fusion.1
  9.5 3.3 %collective-permute-start = (bf16[40,512]{1,0:T(8,128)(2,1)S(1)}, bf16[40,512]{1,0:T(8,128)(2,1)S(1)}, u32[]{:S(2)}, u32[]{:S(2)}) collective-permute-start(bf16[40,512]{1,0:T(8,128)(2,1)S(1)} %bitcast.84), channel_id=1, source_target_pairs={{0,8},{1,9},{2,10},{3,11},{4,12},{5,13},{6,14},{7,15},{8,0},{9,1},... | collective-permute-start | bytes 122888 | tf_op jit(solution)/shard_map/ppermute | solution.py:50
  16.5 3.1 %collective-permute-start.2 = (bf16[80,512]{1,0:T(8,128)(2,1)S(1)}, bf16[80,512]{1,0:T(8,128)(2,1)S(1)}, u32[]{:S(2)}, u32[]{:S(2)}) collective-permute-start(bf16[80,512]{1,0:T(8,128)(2,1)S(1)} %maximum_select_fusion.1), channel_id=1, source_target_pairs={{0,192},{1,193},{2,194},{3,195},{4,196},{5,197},{6,198},{7,199},{8... | collective-permute-start | bytes 245768 | tf_op jit(solution)/shard_map/ppermute | solution.py:50
  19.7 4.4 %collective-permute-start.3 = (bf16[80,512]{1,0:T(8,128)(2,1)S(1)}, bf16[80,512]{1,0:T(8,128)(2,1)S(1)}, u32[]{:S(2)}, u32[]{:S(2)}) collective-permute-start(bf16[80,512]{1,0:T(8,128)(2,1)S(1)} %maximum_select_fusion.1), channel_id=1, source_target_pairs={{0,128},{1,129},{2,130},{3,131},{4,132},{5,133},{6,134},{7,135},{8... | collective-permute-start | bytes 245768 | tf_op jit(solution)/shard_map/ppermute | solution.py:50
  24.2 2.4 %collective-permute-start.7 = (bf16[5,128,256]{2,1,0:T(8,128)(2,1)S(1)}, bf16[5,128,256]{2,1,0:T(8,128)(2,1)S(1)}, u32[]{:S(2)}, u32[]{:S(2)}) collective-permute-start(bf16[5,128,256]{2,1,0:T(8,128)(2,1)S(1)} %get-tuple-element.37), channel_id=1, source_target_pairs={{0,64},{1,65},{2,66},{3,67},{4,68},{5,69},{6,70},{7,71},{8,72},{9,... | collective-permute-start | bytes 983048 | tf_op jit(solution)/shard_map/ppermute | solution.py:50
  29.3 1.5 collective-permute-start.5
  30.8 21.6 %collective-permute-done.6 = bf16[128,1408]{0,1:T(8,128)(2,1)S(1)} collective-permute-done((bf16[128,1408]{0,1:T(8,128)(2,1)S(1)}, bf16[128,1408]{0,1:T(8,128)(2,1)S(1)}, u32[]{:S(2)}, u32[]{:S(2)}) %collective-permute-start.6) | collective-permute-done | bytes 360480 | tf_op jit(solution)/shard_map/ppermute | solution.py:50
  52.4 7.0 %collective-permute-done.8 = bf16[5,128,256]{2,1,0:T(8,128)(2,1)S(1)} collective-permute-done((bf16[5,128,256]{2,1,0:T(8,128)(2,1)S(1)}, bf16[5,128,256]{2,1,0:T(8,128)(2,1)S(1)}, u32[]{:S(2)}, u32[]{:S(2)}) %collective-permute-start.8) | collective-permute-done | bytes 327712 | tf_op jit(solution)/shard_map/ppermute | solution.py:50
  66.7 1.6 copy.40
  73.2 2.1 %collective-permute-start.12 = (bf16[5,128,256]{2,1,0:T(8,128)(2,1)S(1)}, bf16[5,128,256]{2,1,0:T(8,128)(2,1)}, u32[]{:S(2)}, u32[]{:S(2)}) collective-permute-start(bf16[5,128,256]{2,1,0:T(8,128)(2,1)S(1)} %copy-done.7), channel_id=1, source_target_pairs={{0,128},{1,129},{2,130},{3,131},{4,132},{5,133},{6,134},{7,135},{8... | collective-permute-start | bytes 983048 | tf_op jit(solution)/shard_map/ppermute | solution.py:50
  76.0 3.6 %film.1.refs_1_ = bf16[560,512]{1,0:T(8,128)(2,1)S(1)} custom-call(s32[17]{0:T(128)S(1)} %stack.174.order_ref, bf16[16,256,80]{2,1,0:T(8,128)(2,1)S(1)} %bitcast.66, bf16[16,80,512]{2,1,0:T(8,128)(2,1)S(1)} %constant_dynamic-update-slice_fusion.mine_ref, bf16[16,80,512]{2,1,0:T(8,128)(2,1)} %collective-permute-done.11.sibling_ref, ...), custom_call_target="tpu_custom_call" | custom-call | flops 671088640 | bytes 4194304 | tf_op jit(solution)/shard_map/film/pallas_call | solution.py:135
  79.7 13.3 %collective-permute-done.12 = bf16[5,128,256]{2,1,0:T(8,128)(2,1)} collective-permute-done((bf16[5,128,256]{2,1,0:T(8,128)(2,1)S(1)}, bf16[5,128,256]{2,1,0:T(8,128)(2,1)}, u32[]{:S(2)}, u32[]{:S(2)}) %collective-permute-start.12) | collective-permute-done | bytes 327712 | tf_op jit(solution)/shard_map/ppermute | solution.py:50
  92.9 2.5 %collective-permute-start.14 = (bf16[560,512]{1,0:T(8,128)(2,1)S(1)}, bf16[560,512]{1,0:T(8,128)(2,1)S(1)}, u32[]{:S(2)}, u32[]{:S(2)}) collective-permute-start(bf16[560,512]{1,0:T(8,128)(2,1)S(1)} %film.1.refs_1_), channel_id=1, source_target_pairs={{0,1},{1,2},{2,3},{3,0},{4,5},{5,6},{6,7},{7,4},{8,11},{9,8},{10,9... | collective-permute-start | bytes 1720328 | tf_op jit(solution)/shard_map/ppermute | solution.py:50
  95.4 4.6 %first.8.refs_2_ = bf16[8,1024,512]{2,1,0:T(8,128)(2,1)} custom-call(bf16[1024,48]{1,0:T(8,128)(2,1)} %pad.34.refs_0_.window_ref, bf16[560,512]{1,0:T(8,128)(2,1)} %copy-done.2), custom_call_target="tpu_custom_call" | custom-call | flops 50331648 | bytes 2097152 | tf_op jit(solution)/shard_map/first/pallas_call | solution.py:186
  100.0 2.0 %collective-permute-done.14.refs_1_ = bf16[560,512]{1,0:T(8,128)(2,1)S(1)} collective-permute-done((bf16[560,512]{1,0:T(8,128)(2,1)S(1)}, bf16[560,512]{1,0:T(8,128)(2,1)S(1)}, u32[]{:S(2)}, u32[]{:S(2)}) %collective-permute-start.14) | collective-permute-done | bytes 573472 | tf_op jit(solution)/shard_map/ppermute | solution.py:50
  102.1 3.1 %collective-permute-start.16 = (bf16[560,512]{1,0:T(8,128)(2,1)S(1)}, bf16[560,512]{1,0:T(8,128)(2,1)S(1)}, u32[]{:S(2)}, u32[]{:S(2)}) collective-permute-start(bf16[560,512]{1,0:T(8,128)(2,1)S(1)} %collective-permute-done.14.refs_1_), channel_id=1, source_target_pairs={{0,1},{1,2},{2,3},{3,0},{4,5},{5,6},{6,7},{7,4},{8,11},{9,8},{10,9... | collective-permute-start | bytes 1720328 | tf_op jit(solution)/shard_map/ppermute | solution.py:50
  105.2 5.2 %collective-permute-done.13.refs_1_ = bf16[560,512]{1,0:T(8,128)(2,1)S(1)} collective-permute-done((bf16[560,512]{1,0:T(8,128)(2,1)S(1)}, bf16[560,512]{1,0:T(8,128)(2,1)S(1)}, u32[]{:S(2)}, u32[]{:S(2)}) %collective-permute-start.13) | collective-permute-done | bytes 573472 | tf_op jit(solution)/shard_map/ppermute | solution.py:50
  110.4 1.5 collective-permute-start.17
  111.9 4.6 %first.9.refs_2_ = bf16[8,1024,512]{2,1,0:T(8,128)(2,1)} custom-call(bf16[1024,48]{1,0:T(8,128)(2,1)} %pad.34.refs_0_.window_ref, bf16[560,512]{1,0:T(8,128)(2,1)} %copy-done.12, bf16[8,1024,512]{2,1,0:T(8,128)(2,1)} %first.8.refs_2_), custom_call_target="tpu_custom_call", output_to_operand_aliasing={{}: (2, {})} | custom-call | flops 50331648 | bytes 2097152 | tf_op jit(solution)/shard_map/first/pallas_call | solution.py:186
  116.8 2.7 %collective-permute-start.20 = (bf16[5,128,256]{2,1,0:T(8,128)(2,1)S(1)}, bf16[5,128,256]{2,1,0:T(8,128)(2,1)S(1)}, u32[]{:S(2)}, u32[]{:S(2)}) collective-permute-start(bf16[5,128,256]{2,1,0:T(8,128)(2,1)S(1)} %collective-permute-done.17), channel_id=1, source_target_pairs={{0,16},{1,17},{2,18},{3,19},{4,20},{5,21},{6,22},{7,23},{8,56},{9,... | collective-permute-start | bytes 983048 | tf_op jit(solution)/shard_map/ppermute | solution.py:50
  119.5 4.6 %first.10.refs_2_ = bf16[8,1024,512]{2,1,0:T(8,128)(2,1)} custom-call(bf16[1024,48]{1,0:T(8,128)(2,1)} %pad.34.refs_0_.window_ref, bf16[560,512]{1,0:T(8,128)(2,1)} %copy-done.11, bf16[8,1024,512]{2,1,0:T(8,128)(2,1)} %first.9.refs_2_), custom_call_target="tpu_custom_call", output_to_operand_aliasing={{}: (2, {})} | custom-call | flops 50331648 | bytes 2097152 | tf_op jit(solution)/shard_map/first/pallas_call | solution.py:186
  124.9 4.6 %first.11.refs_2_ = bf16[8,1024,512]{2,1,0:T(8,128)(2,1)} custom-call(bf16[1024,48]{1,0:T(8,128)(2,1)} %pad.34.refs_0_.window_ref, bf16[560,512]{1,0:T(8,128)(2,1)} %copy-done.9, bf16[8,1024,512]{2,1,0:T(8,128)(2,1)} %first.10.refs_2_), custom_call_target="tpu_custom_call", output_to_operand_aliasing={{}: (2, {})} | custom-call | flops 50331648 | bytes 2097152 | tf_op jit(solution)/shard_map/first/pallas_call | solution.py:186
  130.3 4.6 %first.12.refs_2_ = bf16[8,1024,512]{2,1,0:T(8,128)(2,1)} custom-call(bf16[1024,48]{1,0:T(8,128)(2,1)} %pad.34.refs_0_.window_ref, bf16[560,512]{1,0:T(8,128)(2,1)} %copy-done.10, bf16[8,1024,512]{2,1,0:T(8,128)(2,1)} %first.11.refs_2_), custom_call_target="tpu_custom_call", output_to_operand_aliasing={{}: (2, {})} | custom-call | flops 50331648 | bytes 2097152 | tf_op jit(solution)/shard_map/first/pallas_call | solution.py:186
  135.6 4.6 %first.13.refs_2_ = bf16[8,1024,512]{2,1,0:T(8,128)(2,1)} custom-call(bf16[1024,48]{1,0:T(8,128)(2,1)} %pad.34.refs_0_.window_ref, bf16[560,512]{1,0:T(8,128)(2,1)} %copy-done.13, bf16[8,1024,512]{2,1,0:T(8,128)(2,1)} %first.12.refs_2_), custom_call_target="tpu_custom_call", output_to_operand_aliasing={{}: (2, {})} | custom-call | flops 50331648 | bytes 2097152 | tf_op jit(solution)/shard_map/first/pallas_call | solution.py:186
  144.2 1.8 collective-permute-start.21
  146.0 4.6 %first.14.refs_1_.refs_2_ = bf16[8,1024,512]{2,1,0:T(8,128)(2,1)} custom-call(bf16[1024,48]{1,0:T(8,128)(2,1)} %pad.34.refs_0_.window_ref, bf16[560,512]{1,0:T(8,128)(2,1)} %copy-done.8, bf16[8,1024,512]{2,1,0:T(8,128)(2,1)} %first.13.refs_2_), custom_call_target="tpu_custom_call", output_to_operand_aliasing={{}: (2, {})} | custom-call | flops 50331648 | bytes 2097152 | tf_op jit(solution)/shard_map/first/pallas_call | solution.py:186
  151.6 13.1 %mid.2.refs_6_ = f32[1024,256]{1,0:T(8,128)} custom-call(s32[10]{0:T(128)} %stack.182.refs_0_, bf16[8,1024,512]{2,1,0:T(8,128)(2,1)} %first.14.refs_1_.refs_2_, bf16[8,5,128,256]{3,2,1,0:T(8,128)(2,1)} %bitcast.71, bf16[8,2,5,128,256]{4,3,2,1,0:T(8,128)(2,1)} %bitcast.68, bf16[4,5,128,256]{3,2,1,0:T(8,128)(2,1)} %copy-done.5, bf16[4,5,128,256]{3,2,1,0:T(8,128)(2,1)} %copy-done.6), custom_call_target="tpu_custom_call" | custom-call | flops 6576668672 | bytes 18350080 | tf_op jit(solution)/shard_map/mid/pallas_call | solution.py:280
  164.7 4.6 %first.15.refs_1_ = bf16[8,1024,512]{2,1,0:T(8,128)(2,1)} custom-call(bf16[1024,48]{1,0:T(8,128)(2,1)} %pad.34.refs_0_.window_ref, bf16[560,512]{1,0:T(8,128)(2,1)} %collective-permute-done.21.refs_1_, bf16[8,1024,512]{2,1,0:T(8,128)(2,1)} %first.14.refs_1_.refs_2_), custom_call_target="tpu_custom_call", output_to_operand_aliasing={{}: (2, {})} | custom-call | flops 50331648 | bytes 2097152 | tf_op jit(solution)/shard_map/first/pallas_call | solution.py:186
  169.4 5.0 %mid.3 = (f32[1024,256]{1,0:T(8,128)}, f32[8,256]{1,0:T(8,128)}) custom-call(s32[4]{0:T(128)} %pad_add_fusion.refs_0_, bf16[8,1024,512]{2,1,0:T(8,128)(2,1)} %first.15.refs_1_, bf16[8,5,128,256]{3,2,1,0:T(8,128)(2,1)} %bitcast.72, bf16[8,2,5,128,256]{4,3,2,1,0:T(8,128)(2,1)} %bitcast.69, bf16[4,5,128,256]{3,2,1,0:T(8,128)(2,1)} %copy-done.5, ...), custom_call_target="tpu_custom_call" | custom-call | flops 939524096 | bytes 2621440 | tf_op jit(solution)/shard_map/mid/pallas_call | solution.py:280
  174.7 3.4 %collective-permute-done.24.other_ref = f32[8,256]{1,0:T(8,128)S(1)} collective-permute-done((f32[8,256]{1,0:T(8,128)}, f32[8,256]{1,0:T(8,128)S(1)}, u32[]{:S(2)}, u32[]{:S(2)}) %collective-permute-start.24) | collective-permute-done | bytes 8224 | tf_op jit(solution)/shard_map/ppermute | solution.py:50
  181.8 4.6 %all-to-all-start = ((f32[16,32,128]{2,1,0:T(8,128)}), f32[16,32,128]{2,1,0:T(8,128)S(1)}, u32[]{:S(2)}, u32[]{:S(2)}) async-start(f32[16,32,128]{2,1,0:T(8,128)} %bitcast.49), calls=%async_computation | async-start | bytes 524288 | tf_op jit(solution)/shard_map/all_to_all | solution.py:464
  186.6 9.4 %all-to-all-done = f32[16,32,128]{2,1,0:T(8,128)S(1)} async-done(((f32[16,32,128]{2,1,0:T(8,128)}), f32[16,32,128]{2,1,0:T(8,128)S(1)}, u32[]{:S(2)}, u32[]{:S(2)}) %all-to-all-start) | async-done | bytes 262176 | tf_op jit(solution)/shard_map/all_to_all | solution.py:464
  (158 shorter events, 31.9 us)
Async XLA Ops:
  7.2 143.4 %all-gather.5.cloned.1.call-start = ((), (), s32[]{:S(2)}) async-start(), calls=%async_computation.1 | async-start | bytes 2949120 | tf_op jit(solution)/shard_map/all_gather | solution.py:364
  9.2 141.4 %all-gather.7.cloned.1.call-start = ((), (), s32[]{:S(2)}) async-start(), calls=%async_computation.2 | async-start | bytes 5898240 | tf_op jit(solution)/shard_map/all_gather | solution.py:386
  9.5 5.7 %collective-permute-start = (bf16[40,512]{1,0:T(8,128)(2,1)S(1)}, bf16[40,512]{1,0:T(8,128)(2,1)S(1)}, u32[]{:S(2)}, u32[]{:S(2)}) collective-permute-start(bf16[40,512]{1,0:T(8,128)(2,1)S(1)} %bitcast.84), channel_id=1, source_target_pairs={{0,8},{1,9},{2,10},{3,11},{4,12},{5,13},{6,14},{7,15},{8,0},{9,1},... | collective-permute-start | bytes 122888 | tf_op jit(solution)/shard_map/ppermute | solution.py:50
  15.2 45.2 %copy-start.15 = (bf16[128,128]{0,1:T(8,128)(2,1)}, bf16[128,128]{0,1:T(8,128)(2,1)S(1)}, u32[]{:S(2)}) copy-start(bf16[128,128]{0,1:T(8,128)(2,1)S(1)} %pad.32) | copy-start | bytes 98308
  15.2 11.3 %collective-permute-start.1 = (bf16[80,512]{1,0:T(8,128)(2,1)S(1)}, bf16[80,512]{1,0:T(8,128)(2,1)S(1)}, u32[]{:S(2)}, u32[]{:S(2)}) collective-permute-start(bf16[80,512]{1,0:T(8,128)(2,1)S(1)} %maximum_select_fusion.1), channel_id=1, source_target_pairs={{0,64},{1,65},{2,66},{3,67},{4,68},{5,69},{6,70},{7,71},{8,72},{9,... | collective-permute-start | bytes 245768 | tf_op jit(solution)/shard_map/ppermute | solution.py:50
  16.5 11.3 %collective-permute-start.2 = (bf16[80,512]{1,0:T(8,128)(2,1)S(1)}, bf16[80,512]{1,0:T(8,128)(2,1)S(1)}, u32[]{:S(2)}, u32[]{:S(2)}) collective-permute-start(bf16[80,512]{1,0:T(8,128)(2,1)S(1)} %maximum_select_fusion.1), channel_id=1, source_target_pairs={{0,192},{1,193},{2,194},{3,195},{4,196},{5,197},{6,198},{7,199},{8... | collective-permute-start | bytes 245768 | tf_op jit(solution)/shard_map/ppermute | solution.py:50
  19.7 8.2 %collective-permute-start.3 = (bf16[80,512]{1,0:T(8,128)(2,1)S(1)}, bf16[80,512]{1,0:T(8,128)(2,1)S(1)}, u32[]{:S(2)}, u32[]{:S(2)}) collective-permute-start(bf16[80,512]{1,0:T(8,128)(2,1)S(1)} %maximum_select_fusion.1), channel_id=1, source_target_pairs={{0,128},{1,129},{2,130},{3,131},{4,132},{5,133},{6,134},{7,135},{8... | collective-permute-start | bytes 245768 | tf_op jit(solution)/shard_map/ppermute | solution.py:50
  24.1 28.4 %collective-permute-start.6 = (bf16[128,1408]{0,1:T(8,128)(2,1)S(1)}, bf16[128,1408]{0,1:T(8,128)(2,1)S(1)}, u32[]{:S(2)}, u32[]{:S(2)}) collective-permute-start(bf16[128,1408]{0,1:T(8,128)(2,1)S(1)} %pad_maximum_fusion.3), channel_id=1, source_target_pairs={{0,64},{1,65},{2,66},{3,67},{4,68},{5,69},{6,70},{7,71},{8,72},{9,... | collective-permute-start | bytes 1081352 | tf_op jit(solution)/shard_map/ppermute | solution.py:50
  24.2 28.3 %collective-permute-start.7 = (bf16[5,128,256]{2,1,0:T(8,128)(2,1)S(1)}, bf16[5,128,256]{2,1,0:T(8,128)(2,1)S(1)}, u32[]{:S(2)}, u32[]{:S(2)}) collective-permute-start(bf16[5,128,256]{2,1,0:T(8,128)(2,1)S(1)} %get-tuple-element.37), channel_id=1, source_target_pairs={{0,64},{1,65},{2,66},{3,67},{4,68},{5,69},{6,70},{7,71},{8,72},{9,... | collective-permute-start | bytes 983048 | tf_op jit(solution)/shard_map/ppermute | solution.py:50
  26.5 32.9 %collective-permute-start.8 = (bf16[5,128,256]{2,1,0:T(8,128)(2,1)S(1)}, bf16[5,128,256]{2,1,0:T(8,128)(2,1)S(1)}, u32[]{:S(2)}, u32[]{:S(2)}) collective-permute-start(bf16[5,128,256]{2,1,0:T(8,128)(2,1)S(1)} %get-tuple-element.37), channel_id=1, source_target_pairs={{0,192},{1,193},{2,194},{3,195},{4,196},{5,197},{6,198},{7,199},{8... | collective-permute-start | bytes 983048 | tf_op jit(solution)/shard_map/ppermute | solution.py:50
  27.8 32.6 %copy-start.24 = (f32[512]{0:T(512)S(1)}, f32[512]{0:T(512)}, u32[]{:S(2)}) copy-start(f32[512]{0:T(512)} %param.25) | copy-start | bytes 6148
  27.8 32.6 %copy-start.20 = (bf16[5,7,512]{2,1,0:T(8,128)(2,1)S(1)}, bf16[5,7,512]{2,1,0:T(8,128)(2,1)}, u32[]{:S(2)}) copy-start(bf16[5,7,512]{2,1,0:T(8,128)(2,1)} %param.21) | copy-start | bytes 107524
  27.9 31.5 %collective-permute-start.4 = (bf16[4,80,512]{2,1,0:T(8,128)(2,1)S(1)}, bf16[4,80,512]{2,1,0:T(8,128)(2,1)S(1)}, u32[]{:S(2)}, u32[]{:S(2)}) collective-permute-start(bf16[4,80,512]{2,1,0:T(8,128)(2,1)S(1)} %pad_maximum_fusion.4), channel_id=1, source_target_pairs={{0,16},{1,17},{2,18},{3,19},{4,20},{5,21},{6,22},{7,23},{8,24},{9,... | collective-permute-start | bytes 983048 | tf_op jit(solution)/shard_map/ppermute | solution.py:50
  29.3 30.2 %collective-permute-start.5 = (bf16[4,80,512]{2,1,0:T(8,128)(2,1)S(1)}, bf16[4,80,512]{2,1,0:T(8,128)(2,1)S(1)}, u32[]{:S(2)}, u32[]{:S(2)}) collective-permute-start(bf16[4,80,512]{2,1,0:T(8,128)(2,1)S(1)} %pad_maximum_fusion.4), channel_id=1, source_target_pairs={{0,48},{1,49},{2,50},{3,51},{4,52},{5,53},{6,54},{7,55},{8,56},{9,... | collective-permute-start | bytes 983048 | tf_op jit(solution)/shard_map/ppermute | solution.py:50
  61.4 8.8 %collective-permute-start.9 = (bf16[2,80,512]{2,1,0:T(8,128)(2,1)}, bf16[2,80,512]{2,1,0:T(8,128)(2,1)}, u32[]{:S(2)}, u32[]{:S(2)}) collective-permute-start(bf16[2,80,512]{2,1,0:T(8,128)(2,1)} %slice.27), channel_id=1, source_target_pairs={{0,16},{1,17},{2,18},{3,19},{4,20},{5,21},{6,22},{7,23},{8,24},{9,... | collective-permute-start | bytes 491528 | tf_op jit(solution)/shard_map/ppermute | solution.py:50
  63.3 7.8 %collective-permute-start.10 = (bf16[2,80,512]{2,1,0:T(8,128)(2,1)}, bf16[2,80,512]{2,1,0:T(8,128)(2,1)}, u32[]{:S(2)}, u32[]{:S(2)}) collective-permute-start(bf16[2,80,512]{2,1,0:T(8,128)(2,1)} %slice.28), channel_id=1, source_target_pairs={{0,48},{1,49},{2,50},{3,51},{4,52},{5,53},{6,54},{7,55},{8,56},{9,... | collective-permute-start | bytes 491528 | tf_op jit(solution)/shard_map/ppermute | solution.py:50
  72.0 4.0 %collective-permute-start.11 = (bf16[16,80,512]{2,1,0:T(8,128)(2,1)S(1)}, bf16[16,80,512]{2,1,0:T(8,128)(2,1)}, u32[]{:S(2)}, u32[]{:S(2)}) collective-permute-start(bf16[16,80,512]{2,1,0:T(8,128)(2,1)S(1)} %constant_dynamic-update-slice_fusion.mine_ref), channel_id=1, source_target_pairs={{0,8},{1,9},{2,10},{3,11},{4,12},{5,13},{6,14},{7,15},{8,0},{9,1},... | collective-permute-start | bytes 3932168 | tf_op jit(solution)/shard_map/ppermute | solution.py:50
  73.2 19.7 %collective-permute-start.12 = (bf16[5,128,256]{2,1,0:T(8,128)(2,1)S(1)}, bf16[5,128,256]{2,1,0:T(8,128)(2,1)}, u32[]{:S(2)}, u32[]{:S(2)}) collective-permute-start(bf16[5,128,256]{2,1,0:T(8,128)(2,1)S(1)} %copy-done.7), channel_id=1, source_target_pairs={{0,128},{1,129},{2,130},{3,131},{4,132},{5,133},{6,134},{7,135},{8... | collective-permute-start | bytes 983048 | tf_op jit(solution)/shard_map/ppermute | solution.py:50
  92.9 9.1 %collective-permute-start.14 = (bf16[560,512]{1,0:T(8,128)(2,1)S(1)}, bf16[560,512]{1,0:T(8,128)(2,1)S(1)}, u32[]{:S(2)}, u32[]{:S(2)}) collective-permute-start(bf16[560,512]{1,0:T(8,128)(2,1)S(1)} %film.1.refs_1_), channel_id=1, source_target_pairs={{0,1},{1,2},{2,3},{3,0},{4,5},{5,6},{6,7},{7,4},{8,11},{9,8},{10,9... | collective-permute-start | bytes 1720328 | tf_op jit(solution)/shard_map/ppermute | solution.py:50
  95.4 14.9 %collective-permute-start.13 = (bf16[560,512]{1,0:T(8,128)(2,1)S(1)}, bf16[560,512]{1,0:T(8,128)(2,1)S(1)}, u32[]{:S(2)}, u32[]{:S(2)}) collective-permute-start(bf16[560,512]{1,0:T(8,128)(2,1)S(1)} %film.1.refs_1_), channel_id=1, source_target_pairs={{0,4},{1,5},{2,6},{3,7},{4,0},{5,1},{6,2},{7,3},{8,12},{9,13},{10,... | collective-permute-start | bytes 1720328 | tf_op jit(solution)/shard_map/ppermute | solution.py:50
  102.1 22.0 %collective-permute-start.16 = (bf16[560,512]{1,0:T(8,128)(2,1)S(1)}, bf16[560,512]{1,0:T(8,128)(2,1)S(1)}, u32[]{:S(2)}, u32[]{:S(2)}) collective-permute-start(bf16[560,512]{1,0:T(8,128)(2,1)S(1)} %collective-permute-done.14.refs_1_), channel_id=1, source_target_pairs={{0,1},{1,2},{2,3},{3,0},{4,5},{5,6},{6,7},{7,4},{8,11},{9,8},{10,9... | collective-permute-start | bytes 1720328 | tf_op jit(solution)/shard_map/ppermute | solution.py:50
  110.3 19.1 %collective-permute-start.15 = (bf16[560,512]{1,0:T(8,128)(2,1)S(1)}, bf16[560,512]{1,0:T(8,128)(2,1)S(1)}, u32[]{:S(2)}, u32[]{:S(2)}) collective-permute-start(bf16[560,512]{1,0:T(8,128)(2,1)S(1)} %collective-permute-done.13.refs_1_), channel_id=1, source_target_pairs={{0,1},{1,2},{2,3},{3,0},{4,5},{5,6},{6,7},{7,4},{8,11},{9,8},{10,9... | collective-permute-start | bytes 1720328 | tf_op jit(solution)/shard_map/ppermute | solution.py:50
  110.4 6.4 %collective-permute-start.17 = (bf16[5,128,256]{2,1,0:T(8,128)(2,1)}, bf16[5,128,256]{2,1,0:T(8,128)(2,1)S(1)}, u32[]{:S(2)}, u32[]{:S(2)}) collective-permute-start(bf16[5,128,256]{2,1,0:T(8,128)(2,1)} %collective-permute-done.12), channel_id=1, source_target_pairs={{0,16},{1,17},{2,18},{3,19},{4,20},{5,21},{6,22},{7,23},{8,56},{9,... | collective-permute-start | bytes 983048 | tf_op jit(solution)/shard_map/ppermute | solution.py:50
  116.8 12.7 %collective-permute-start.20 = (bf16[5,128,256]{2,1,0:T(8,128)(2,1)S(1)}, bf16[5,128,256]{2,1,0:T(8,128)(2,1)S(1)}, u32[]{:S(2)}, u32[]{:S(2)}) collective-permute-start(bf16[5,128,256]{2,1,0:T(8,128)(2,1)S(1)} %collective-permute-done.17), channel_id=1, source_target_pairs={{0,16},{1,17},{2,18},{3,19},{4,20},{5,21},{6,22},{7,23},{8,56},{9,... | collective-permute-start | bytes 983048 | tf_op jit(solution)/shard_map/ppermute | solution.py:50
  124.1 10.7 %collective-permute-start.19 = (bf16[560,512]{1,0:T(8,128)(2,1)S(1)}, bf16[560,512]{1,0:T(8,128)(2,1)S(1)}, u32[]{:S(2)}, u32[]{:S(2)}) collective-permute-start(bf16[560,512]{1,0:T(8,128)(2,1)S(1)} %collective-permute-done.16.refs_1_), channel_id=1, source_target_pairs={{0,1},{1,2},{2,3},{3,0},{4,5},{5,6},{6,7},{7,4},{8,11},{9,8},{10,9... | collective-permute-start | bytes 1720328 | tf_op jit(solution)/shard_map/ppermute | solution.py:50
  129.5 10.8 %collective-permute-start.18 = (bf16[560,512]{1,0:T(8,128)(2,1)S(1)}, bf16[560,512]{1,0:T(8,128)(2,1)S(1)}, u32[]{:S(2)}, u32[]{:S(2)}) collective-permute-start(bf16[560,512]{1,0:T(8,128)(2,1)S(1)} %collective-permute-done.15.refs_1_), channel_id=1, source_target_pairs={{0,1},{1,2},{2,3},{3,0},{4,5},{5,6},{6,7},{7,4},{8,11},{9,8},{10,9... | collective-permute-start | bytes 1720328 | tf_op jit(solution)/shard_map/ppermute | solution.py:50
  129.5 10.8 %collective-permute-start.22 = (bf16[5,128,256]{2,1,0:T(8,128)(2,1)S(1)}, bf16[5,128,256]{2,1,0:T(8,128)(2,1)S(1)}, u32[]{:S(2)}, u32[]{:S(2)}) collective-permute-start(bf16[5,128,256]{2,1,0:T(8,128)(2,1)S(1)} %collective-permute-done.20), channel_id=1, source_target_pairs={{0,16},{1,17},{2,18},{3,19},{4,20},{5,21},{6,22},{7,23},{8,56},{9,... | collective-permute-start | bytes 983048 | tf_op jit(solution)/shard_map/ppermute | solution.py:50
  141.6 8.9 %collective-permute-start.23 = (bf16[4,5,128,256]{3,2,1,0:T(8,128)(2,1)S(1)}, bf16[4,5,128,256]{3,2,1,0:T(8,128)(2,1)S(1)}, u32[]{:S(2)}, u32[]{:S(2)}) collective-permute-start(bf16[4,5,128,256]{3,2,1,0:T(8,128)(2,1)S(1)} %pad_maximum_fusion.refs_4_), channel_id=1, source_target_pairs={{0,8},{1,9},{2,10},{3,11},{4,12},{5,13},{6,14},{7,15},{8,0},{9,1},... | collective-permute-start | bytes 3932168 | tf_op jit(solution)/shard_map/ppermute | solution.py:50
  144.2 20.5 %collective-permute-start.21 = (bf16[560,512]{1,0:T(8,128)(2,1)}, bf16[560,512]{1,0:T(8,128)(2,1)}, u32[]{:S(2)}, u32[]{:S(2)}) collective-permute-start(bf16[560,512]{1,0:T(8,128)(2,1)} %copy-done.8), channel_id=1, source_target_pairs={{0,1},{1,2},{2,3},{3,0},{4,5},{5,6},{6,7},{7,4},{8,11},{9,8},{10,9... | collective-permute-start | bytes 1720328 | tf_op jit(solution)/shard_map/ppermute | solution.py:50
  174.5 3.7 %collective-permute-start.24 = (f32[8,256]{1,0:T(8,128)}, f32[8,256]{1,0:T(8,128)S(1)}, u32[]{:S(2)}, u32[]{:S(2)}) collective-permute-start(f32[8,256]{1,0:T(8,128)} %get-tuple-element.69.own_ref), channel_id=1, source_target_pairs={{0,64},{1,65},{2,66},{3,67},{4,68},{5,69},{6,70},{7,71},{8,72},{9,... | collective-permute-start | bytes 24584 | tf_op jit(solution)/shard_map/ppermute | solution.py:50
  174.6 21.4 %copy-start.19 = (f32[128,28]{0,1:T(8,128)S(1)}, f32[128,28]{0,1:T(8,128)}, u32[]{:S(2)}) copy-start(f32[128,28]{0,1:T(8,128)} %param.14) | copy-start | bytes 43012
  181.8 14.2 %all-to-all-start = ((f32[16,32,128]{2,1,0:T(8,128)}), f32[16,32,128]{2,1,0:T(8,128)S(1)}, u32[]{:S(2)}, u32[]{:S(2)}) async-start(f32[16,32,128]{2,1,0:T(8,128)} %bitcast.49), calls=%async_computation | async-start | bytes 524288 | tf_op jit(solution)/shard_map/all_to_all | solution.py:464
  (27 other events, 163.1 us)
Sparse Core Ops, SparseCore 0:
  9.9 39.0 all-gather.4
  60.5 37.6 all-gather.6
